TPU v7x, 256 devices: a whole 4x4x8 slice. The times are simulated.
256 devices in a mesh: section: 4 (over x), seq: 8 (over y, core), tensor: 8 (over z).
Axes of the slice: x: 4, y: 4, z: 8, core: 2. Of those that a mesh axis runs over, the one named last changes fastest.
Arguments:
- prompt_query: bfloat16 [4, 4096, 8192], P('section', 'seq', 'tensor'), may hold values from -137 to 137
- prompt_keys: bfloat16 [4, 4096, 1024], P('section', 'seq', 'tensor'), may hold values from -4.6 to 4.6
- prompt_values: bfloat16 [4, 4096, 1024], P('section', 'seq', 'tensor'), may hold values from -6 to 6
- page_owner: int32 [4, 128], P('section', 'seq'), may hold values from 0 to 31, as said below
- pool_keys: bfloat16 [8192, 32, 1024], P(('section', 'seq'), None, 'tensor'), may hold values from -4.6 to 4.6
- pool_values: bfloat16 [8192, 32, 1024], P(('section', 'seq'), None, 'tensor'), may hold values from -6 to 6
- step_query: bfloat16 [512, 4, 8192], P(('section', 'seq'), None, 'tensor'), may hold values from -137 to 137
- step_keys: bfloat16 [512, 4, 1024], P(('section', 'seq'), None, 'tensor'), may hold values from -4.5 to 4.5
- step_values: bfloat16 [512, 4, 1024], P(('section', 'seq'), None, 'tensor'), may hold values from -6 to 6
- page_table: int32 [512, 64], P(('section', 'seq')), may hold values from 0 to 287, as said below
- context_len: int32 [512], P(('section', 'seq')), may hold values from 2 to 2048, as said below
Outputs:
- prefill_out: bfloat16 [4, 4096, 8192], P('section', 'seq', 'tensor')
- decode_out: bfloat16 [512, 4, 8192], P(('section', 'seq'), None, 'tensor')
Inputs may be any that keep to these rules, and one draw needn't show every extreme that they name: `page_owner`: no decode device takes more than 1 pages of one block; some decode device takes exactly 1 pages of every block. `page_table`: an entry 256 + b + k appears only where block b sends more than k pages to the request's decode device. Every entry, used or not, follows this rule. The first entry of every row is below 256. `context_len`: some request has exactly 2048 cached tokens.
All inputs are finite; a program needn't handle non-finite values.
Results may differ from a plain program's by a relative error of at most 0.0045.
Values may be sent and summed in bfloat16 or wider, within the bound.
A program may use at most 192 MiB of HBM per device.

v0:
```python
import math

import jax
import jax.numpy as jnp
from jax import lax
from jax.sharding import PartitionSpec as P

HEAD_DIM = 128
PAGE = 32
MAXPG = 64
STEPS = 4


masked_score = -1e30


def online_update(state, scores, valid, values_block, pattern):
    maximum, total, accum = state
    scores = jnp.where(valid, scores, masked_score)
    fresh = jnp.maximum(maximum, jnp.max(scores, axis=-1))
    factor = jnp.exp(maximum - fresh)
    weights = jnp.where(valid, jnp.exp(scores - fresh[..., None]), 0.0)
    total = total * factor + jnp.sum(weights, axis=-1)
    product = jnp.einsum(
        pattern, weights.astype(jnp.bfloat16), values_block, preferred_element_type=jnp.float32
    )
    accum = accum * factor[..., None] + product
    return (fresh, total, accum)


def span_attend(query, positions, state, keys, values):
    rows = keys.shape[0]
    kv_local = query.shape[1]
    width = math.gcd(rows, 512)
    scale = 1.0 / math.sqrt(HEAD_DIM)

    def span_advance(index, current):
        key_block = lax.dynamic_slice_in_dim(keys, index * width, width, 0).reshape(
            width, kv_local, HEAD_DIM
        )
        value_block = lax.dynamic_slice_in_dim(values, index * width, width, 0).reshape(
            width, kv_local, HEAD_DIM
        )
        scores = (
            jnp.einsum("tkgd,skd->tkgs", query, key_block, preferred_element_type=jnp.float32)
            * scale
        )
        key_rows = index * width + jnp.arange(width, dtype=jnp.int32)
        valid = (key_rows[None, :] <= positions[:, None]) & (key_rows[None, :] >= 0)
        return online_update(
            current, scores, valid[:, None, None, :], value_block, "tkgs,skd->tkgd"
        )

    return lax.fori_loop(0, rows // width, span_advance, state)


def on_device(
    prompt_query,
    prompt_keys,
    prompt_values,
    page_owner,
    pool_keys,
    pool_values,
    step_query,
    step_keys,
    step_values,
    page_table,
    context_len,
):
    tokens_here = prompt_query.shape[1]
    feature = prompt_keys.shape[2]
    kv_local = feature // HEAD_DIM
    group = prompt_query.shape[2] // feature
    scale = 1.0 / math.sqrt(HEAD_DIM)
    query = prompt_query[0].reshape(tokens_here, kv_local, group, HEAD_DIM)
    row_start = lax.axis_index("seq") * tokens_here
    positions = row_start + jnp.arange(tokens_here, dtype=jnp.int32)
    initial = (
        jnp.full((tokens_here, kv_local, group), masked_score, jnp.float32),
        jnp.zeros((tokens_here, kv_local, group), jnp.float32),
        jnp.zeros((tokens_here, kv_local, group, HEAD_DIM), jnp.float32),
    )
    state = span_attend(
        query,
        positions,
        initial,
        lax.all_gather(prompt_keys, "seq", axis=1, tiled=True)[0],
        lax.all_gather(prompt_values, "seq", axis=1, tiled=True)[0],
    )
    prefill_out = (
        (state[2] / state[1][..., None])
        .reshape(1, tokens_here, group * feature)
        .astype(jnp.bfloat16)
    )
    per_dev = tokens_here // PAGE
    decoders = lax.axis_size(("section", "seq"))
    capacity = (per_dev + decoders - 1) // decoders
    pages = jnp.stack(
        [
            prompt_keys[0].reshape(per_dev, PAGE * feature),
            prompt_values[0].reshape(per_dev, PAGE * feature),
        ],
        1,
    ).reshape(per_dev, 2 * PAGE * feature)
    owners = page_owner[0]
    page_ids = jnp.arange(per_dev, dtype=jnp.int32)
    same_owner = owners[None, :] == owners[:, None]
    before = page_ids[None, :] < page_ids[:, None]
    order_rank = jnp.sum((same_owner & before).astype(jnp.int32), axis=1)
    targets = jnp.arange(decoders * capacity, dtype=jnp.int32)
    select = (
        (owners[None, :] == targets[:, None] // capacity)
        & (order_rank[None, :] == targets[:, None] % capacity)
    ).astype(jnp.bfloat16)
    outgoing = jnp.dot(select, pages, preferred_element_type=jnp.float32).astype(jnp.bfloat16)
    arrived = lax.all_to_all(outgoing, ("section", "seq"), split_axis=0, concat_axis=0, tiled=True)
    arrived = arrived.reshape(decoders * capacity, 2, PAGE, feature)
    all_keys = jnp.concatenate([pool_keys, arrived[:, 0]], 0)
    all_values = jnp.concatenate([pool_values, arrived[:, 1]], 0)
    requests = step_query.shape[0]
    step_q = step_query.reshape(requests, STEPS, kv_local, group, HEAD_DIM)
    new_keys = step_keys.reshape(requests, STEPS, kv_local, HEAD_DIM)
    new_values = step_values.reshape(requests, STEPS, kv_local, HEAD_DIM)
    start_state = (
        jnp.full((requests, STEPS, kv_local, group), masked_score, jnp.float32),
        jnp.zeros((requests, STEPS, kv_local, group), jnp.float32),
        jnp.zeros((requests, STEPS, kv_local, group, HEAD_DIM), jnp.float32),
    )
    own_scores = (
        jnp.einsum("rtkgd,rukd->rtkgu", step_q, new_keys, preferred_element_type=jnp.float32)
        * scale
    )
    own_valid = (jnp.arange(STEPS)[None, :] <= jnp.arange(STEPS)[:, None])[None, :, None, None, :]
    state = online_update(start_state, own_scores, own_valid, new_values, "rtkgu,rukd->rtkgd")
    block_pages = math.gcd(MAXPG, 8)
    window = block_pages * PAGE

    def body_advance(index, current):
        entries = lax.dynamic_slice_in_dim(page_table, index * block_pages, block_pages, 1)
        key_block = all_keys[entries].reshape(requests, window, kv_local, HEAD_DIM)
        value_block = all_values[entries].reshape(requests, window, kv_local, HEAD_DIM)
        scores = (
            jnp.einsum("rtkgd,rskd->rtkgs", step_q, key_block, preferred_element_type=jnp.float32)
            * scale
        )
        rows = index * window + jnp.arange(window, dtype=jnp.int32)
        valid = (rows[None, :] < context_len[:, None])[:, None, None, None, :]
        return online_update(current, scores, valid, value_block, "rtkgs,rskd->rtkgd")

    state = lax.fori_loop(0, MAXPG // block_pages, body_advance, state)
    decode_out = (
        (state[2] / state[1][..., None])
        .reshape(requests, STEPS, group * feature)
        .astype(jnp.bfloat16)
    )
    return (prefill_out, decode_out)


def solution(mesh):
    in_specs = (
        P("section", "seq", "tensor"),
        P("section", "seq", "tensor"),
        P("section", "seq", "tensor"),
        P("section", "seq"),
        P(("section", "seq"), None, "tensor"),
        P(("section", "seq"), None, "tensor"),
        P(("section", "seq"), None, "tensor"),
        P(("section", "seq"), None, "tensor"),
        P(("section", "seq"), None, "tensor"),
        P(("section", "seq"), None),
        P(("section", "seq")),
    )
    out_specs = (P("section", "seq", "tensor"), P(("section", "seq"), None, "tensor"))
    return jax.shard_map(
        on_device, mesh=mesh, in_specs=in_specs, out_specs=out_specs, check_vma=False
    )
```

profile of v0, /device:TPU:120, one launch (start us, length us, event | category | flops | bytes accessed | tf_op | source)
XLA Modules:
  0.0 246.5 jit_solution(12922675341606113183)
XLA Ops:
  15.8 7.3 %all-to-all-start = ((bf16[32,2,4096]{2,1,0:T(2,128)(2,1)}), bf16[32,2,4096]{2,1,0:T(2,128)(2,1)S(1)}, u32[]{:S(2)}, u32[]{:S(2)}) async-start(bf16[32,2,4096]{2,1,0:T(2,128)(2,1)} %reshape.362), calls=%async_computation | async-start | bytes 1048576 | tf_op jit(solution)/shard_map/all_to_all | solution.py:116
  28.5 4.3 %all-to-all-done = bf16[32,2,4096]{2,1,0:T(2,128)(2,1)S(1)} async-done(((bf16[32,2,4096]{2,1,0:T(2,128)(2,1)}), bf16[32,2,4096]{2,1,0:T(2,128)(2,1)S(1)}, u32[]{:S(2)}, u32[]{:S(2)}) %all-to-all-start) | async-done | bytes 524320 | tf_op jit(solution)/shard_map/all_to_all | solution.py:116
  33.3 3.2 %reduce.14 = bf16[32,8192]{1,0:T(8,128)(2,1)S(1)} reduce(bf16[32,1,8192]{2,1,0:T(2,128)(2,1)S(1)} %reshape.363, bf16[]{:T(256)} %constant.173), dimensions={1}, to_apply=%all_to_all.7.reduce_sub_computation | reduce | bytes 1048578 | tf_op jit(solution)/shard_map/all_to_all | solution.py:116
  38.1 3.6 %pad_maximum_fusion = (bf16[288,32,128]{2,1,0:T(8,128)(2,1)}, bf16[288,32,128]{2,1,0:T(8,128)(2,1)}) fusion(bf16[32,32,128]{2,1,0:T(8,128)(2,1)S(1)} %get-tuple-element.408, bf16[256,32,128]{2,1,0:T(8,128)(2,1)S(1)} %copy-done.4, bf16[32,32,128]{2,1,0:T(8,128)(2,1)S(1)} %get-tuple-element.407, bf16[256,32,128]{2,1,0:T(8,128)(2,1)} %param.20), kind=kLoop, calls=%fused_computation.58 | loop fusion | flops 2359296 | bytes 9437184 | tf_op jit(solution)/shard_map/concatenate | solution.py:118
  41.7 57.3 %while.35 = (s32[]{:T(128)}, f32[16,4,1,8]{3,1,0,2:T(4,128)S(1)}, f32[16,4,1,8]{3,1,0,2:T(4,128)S(1)}, f32[16,4,1,8,128]{4,3,1,0,2:T(8,128)}, s32[16]{0:T(128)S(...) while((s32[]{:T(128)}, f32[16,4,1,8]{3,1,0,2:T(4,128)S(1)}, ...), condition=%wide.region_10.11_spmd, body=%wide.region_7.10_spmd.sunk | while | flops 68426888 | bytes 10676039 | solution.py:150
  56.2 2.5 %gather_fusion = bf16[128,32,128]{2,1,0:T(8,128)(2,1)S(1)} fusion(bf16[288,32,128]{2,1,0:T(8,128)(2,1)} %get-tuple-element.610, s32[1024]{0:T(1024)S(1)} %pad_clamp_fusion.2), kind=kCustom, calls=%fused_computation.clone.1 | custom fusion | bytes 2097664 | tf_op jit(solution)/shard_map/while/body/eval_jaxpr/gather | solution.py:140
  59.8 2.5 %gather_fusion.1 = bf16[128,32,128]{2,1,0:T(8,128)(2,1)S(1)} fusion(bf16[288,32,128]{2,1,0:T(8,128)(2,1)} %get-tuple-element.612, s32[1024]{0:T(1024)S(1)} %pad_clamp_fusion.2), kind=kCustom, calls=%fused_computation.1.clone.1 | custom fusion | bytes 2097664 | tf_op jit(solution)/shard_map/while/body/eval_jaxpr/gather | solution.py:141
  100.9 135.6 %while.36 = (s32[]{:T(128)}, f32[512,1,8]{0,2,1:T(8,128)S(1)}, f32[512,1,8]{0,2,1:T(8,128)S(1)}, f32[512,1,8,128]{0,3,2,1:T(8,128)}, bf16[4096,128]{1,0:T(8,128)...) while((s32[]{:T(128)}, f32[512,1,8]{0,2,1:T(8,128)S(1)}, ...), condition=%wide.region_3.4_spmd.clone, body=%wide.region_0.3_spmd.clone.sunk | while | flops 1103128576 | bytes 82322720 | solution.py:54
  101.1 5.7 %fusion.85 = (f32[512,8]{0,1:T(8,128)S(1)}, f32[512,512,8]{1,0,2:T(8,128)}) fusion(pred[512,512]{0,1:T(8,128)(4,1)S(1)} %compare_and_fusion.2, bf16[512,1,8,128]{3,0,2,1:T(8,128)(2,1)S(1)} %get-tuple-element.569, bf16[4096,128]{1,0:T(8,128)(2,1)} %get-tuple-element.568, s32[]{:T(128)S(6)} %select_n.145), kind=kOutput, calls=%fused_computation.28.clone.1 | convolution fusion | flops 543158272 | bytes 9846788 | tf_op jit(solution)/shard_map/while/body/eval_jaxpr/tkgd,skd->tkgs/dot_general | solution.py:45
  106.9 4.6 %fusion.87 = f32[512,8]{0,1:T(8,128)S(1)} fusion(f32[512,512,8]{1,0,2:T(8,128)} %get-tuple-element.538, f32[512,8]{0,1:T(8,128)S(1)} %bitcast.195, pred[512,512]{0,1:T(8,128)(4,1)S(1)} %compare_and_fusion.2), kind=kLoop, calls=%fused_computation.30.clone.1 | loop fusion | flops 10481664 | bytes 8683520 | tf_op jit(solution)/shard_map/while/body/eval_jaxpr/reduce_sum | solution.py:23
  112.7 3.7 %bitcast_add_fusion.9 = f32[512,1,8,128]{0,3,2,1:T(8,128)S(1)} fusion(f32[512,1,8,128]{0,3,2,1:T(8,128)S(1)} %copy-done.2, f32[512,512,8]{1,0,2:T(8,128)S(1)} %copy-done.1, f32[512,8]{0,1:T(8,128)S(1)} %bitcast.196, pred[512,512]{0,1:T(8,128)(4,1)S(1)} %compare_and_fusion.2, f32[512,8]{0,1:T(8,128)S(1)} %get-tuple-element.539, pred[]{:T(512)S(6)} %compare.7, ...), kind=kOutput, calls=%fused_computation.34.clone.1 | convolution fusion | flops 548929536 | bytes 13008901 | tf_op jit(solution)/shard_map/while/body/eval_jaxpr/tkgs,skd->tkgd/dot_general | solution.py:24
  118.1 5.8 %fusion.85 = (f32[512,8]{0,1:T(8,128)S(1)}, f32[512,512,8]{1,0,2:T(8,128)}) fusion(pred[512,512]{0,1:T(8,128)(4,1)S(1)} %compare_and_fusion.2, bf16[512,1,8,128]{3,0,2,1:T(8,128)(2,1)S(1)} %get-tuple-element.569, bf16[4096,128]{1,0:T(8,128)(2,1)} %get-tuple-element.568, s32[]{:T(128)S(6)} %select_n.145), kind=kOutput, calls=%fused_computation.28.clone.1 | convolution fusion | flops 543158272 | bytes 9846788 | tf_op jit(solution)/shard_map/while/body/eval_jaxpr/tkgd,skd->tkgs/dot_general | solution.py:45
  123.9 4.6 %fusion.87 = f32[512,8]{0,1:T(8,128)S(1)} fusion(f32[512,512,8]{1,0,2:T(8,128)} %get-tuple-element.538, f32[512,8]{0,1:T(8,128)S(1)} %bitcast.195, pred[512,512]{0,1:T(8,128)(4,1)S(1)} %compare_and_fusion.2), kind=kLoop, calls=%fused_computation.30.clone.1 | loop fusion | flops 10481664 | bytes 8683520 | tf_op jit(solution)/shard_map/while/body/eval_jaxpr/reduce_sum | solution.py:23
  129.7 3.7 %bitcast_add_fusion.9 = f32[512,1,8,128]{0,3,2,1:T(8,128)S(1)} fusion(f32[512,1,8,128]{0,3,2,1:T(8,128)S(1)} %copy-done.2, f32[512,512,8]{1,0,2:T(8,128)S(1)} %copy-done.1, f32[512,8]{0,1:T(8,128)S(1)} %bitcast.196, pred[512,512]{0,1:T(8,128)(4,1)S(1)} %compare_and_fusion.2, f32[512,8]{0,1:T(8,128)S(1)} %get-tuple-element.539, pred[]{:T(512)S(6)} %compare.7, ...), kind=kOutput, calls=%fused_computation.34.clone.1 | convolution fusion | flops 548929536 | bytes 13008901 | tf_op jit(solution)/shard_map/while/body/eval_jaxpr/tkgs,skd->tkgd/dot_general | solution.py:24
  135.0 5.8 %fusion.85 = (f32[512,8]{0,1:T(8,128)S(1)}, f32[512,512,8]{1,0,2:T(8,128)}) fusion(pred[512,512]{0,1:T(8,128)(4,1)S(1)} %compare_and_fusion.2, bf16[512,1,8,128]{3,0,2,1:T(8,128)(2,1)S(1)} %get-tuple-element.569, bf16[4096,128]{1,0:T(8,128)(2,1)} %get-tuple-element.568, s32[]{:T(128)S(6)} %select_n.145), kind=kOutput, calls=%fused_computation.28.clone.1 | convolution fusion | flops 543158272 | bytes 9846788 | tf_op jit(solution)/shard_map/while/body/eval_jaxpr/tkgd,skd->tkgs/dot_general | solution.py:45
  140.8 4.6 %fusion.87 = f32[512,8]{0,1:T(8,128)S(1)} fusion(f32[512,512,8]{1,0,2:T(8,128)} %get-tuple-element.538, f32[512,8]{0,1:T(8,128)S(1)} %bitcast.195, pred[512,512]{0,1:T(8,128)(4,1)S(1)} %compare_and_fusion.2), kind=kLoop, calls=%fused_computation.30.clone.1 | loop fusion | flops 10481664 | bytes 8683520 | tf_op jit(solution)/shard_map/while/body/eval_jaxpr/reduce_sum | solution.py:23
  146.6 3.7 %bitcast_add_fusion.9 = f32[512,1,8,128]{0,3,2,1:T(8,128)S(1)} fusion(f32[512,1,8,128]{0,3,2,1:T(8,128)S(1)} %copy-done.2, f32[512,512,8]{1,0,2:T(8,128)S(1)} %copy-done.1, f32[512,8]{0,1:T(8,128)S(1)} %bitcast.196, pred[512,512]{0,1:T(8,128)(4,1)S(1)} %compare_and_fusion.2, f32[512,8]{0,1:T(8,128)S(1)} %get-tuple-element.539, pred[]{:T(512)S(6)} %compare.7, ...), kind=kOutput, calls=%fused_computation.34.clone.1 | convolution fusion | flops 548929536 | bytes 13008901 | tf_op jit(solution)/shard_map/while/body/eval_jaxpr/tkgs,skd->tkgd/dot_general | solution.py:24
  152.0 5.8 %fusion.85 = (f32[512,8]{0,1:T(8,128)S(1)}, f32[512,512,8]{1,0,2:T(8,128)}) fusion(pred[512,512]{0,1:T(8,128)(4,1)S(1)} %compare_and_fusion.2, bf16[512,1,8,128]{3,0,2,1:T(8,128)(2,1)S(1)} %get-tuple-element.569, bf16[4096,128]{1,0:T(8,128)(2,1)} %get-tuple-element.568, s32[]{:T(128)S(6)} %select_n.145), kind=kOutput, calls=%fused_computation.28.clone.1 | convolution fusion | flops 543158272 | bytes 9846788 | tf_op jit(solution)/shard_map/while/body/eval_jaxpr/tkgd,skd->tkgs/dot_general | solution.py:45
  157.8 4.6 %fusion.87 = f32[512,8]{0,1:T(8,128)S(1)} fusion(f32[512,512,8]{1,0,2:T(8,128)} %get-tuple-element.538, f32[512,8]{0,1:T(8,128)S(1)} %bitcast.195, pred[512,512]{0,1:T(8,128)(4,1)S(1)} %compare_and_fusion.2), kind=kLoop, calls=%fused_computation.30.clone.1 | loop fusion | flops 10481664 | bytes 8683520 | tf_op jit(solution)/shard_map/while/body/eval_jaxpr/reduce_sum | solution.py:23
  163.6 3.7 %bitcast_add_fusion.9 = f32[512,1,8,128]{0,3,2,1:T(8,128)S(1)} fusion(f32[512,1,8,128]{0,3,2,1:T(8,128)S(1)} %copy-done.2, f32[512,512,8]{1,0,2:T(8,128)S(1)} %copy-done.1, f32[512,8]{0,1:T(8,128)S(1)} %bitcast.196, pred[512,512]{0,1:T(8,128)(4,1)S(1)} %compare_and_fusion.2, f32[512,8]{0,1:T(8,128)S(1)} %get-tuple-element.539, pred[]{:T(512)S(6)} %compare.7, ...), kind=kOutput, calls=%fused_computation.34.clone.1 | convolution fusion | flops 548929536 | bytes 13008901 | tf_op jit(solution)/shard_map/while/body/eval_jaxpr/tkgs,skd->tkgd/dot_general | solution.py:24
  168.9 5.8 %fusion.85 = (f32[512,8]{0,1:T(8,128)S(1)}, f32[512,512,8]{1,0,2:T(8,128)}) fusion(pred[512,512]{0,1:T(8,128)(4,1)S(1)} %compare_and_fusion.2, bf16[512,1,8,128]{3,0,2,1:T(8,128)(2,1)S(1)} %get-tuple-element.569, bf16[4096,128]{1,0:T(8,128)(2,1)} %get-tuple-element.568, s32[]{:T(128)S(6)} %select_n.145), kind=kOutput, calls=%fused_computation.28.clone.1 | convolution fusion | flops 543158272 | bytes 9846788 | tf_op jit(solution)/shard_map/while/body/eval_jaxpr/tkgd,skd->tkgs/dot_general | solution.py:45
  174.7 4.6 %fusion.87 = f32[512,8]{0,1:T(8,128)S(1)} fusion(f32[512,512,8]{1,0,2:T(8,128)} %get-tuple-element.538, f32[512,8]{0,1:T(8,128)S(1)} %bitcast.195, pred[512,512]{0,1:T(8,128)(4,1)S(1)} %compare_and_fusion.2), kind=kLoop, calls=%fused_computation.30.clone.1 | loop fusion | flops 10481664 | bytes 8683520 | tf_op jit(solution)/shard_map/while/body/eval_jaxpr/reduce_sum | solution.py:23
  180.5 3.7 %bitcast_add_fusion.9 = f32[512,1,8,128]{0,3,2,1:T(8,128)S(1)} fusion(f32[512,1,8,128]{0,3,2,1:T(8,128)S(1)} %copy-done.2, f32[512,512,8]{1,0,2:T(8,128)S(1)} %copy-done.1, f32[512,8]{0,1:T(8,128)S(1)} %bitcast.196, pred[512,512]{0,1:T(8,128)(4,1)S(1)} %compare_and_fusion.2, f32[512,8]{0,1:T(8,128)S(1)} %get-tuple-element.539, pred[]{:T(512)S(6)} %compare.7, ...), kind=kOutput, calls=%fused_computation.34.clone.1 | convolution fusion | flops 548929536 | bytes 13008901 | tf_op jit(solution)/shard_map/while/body/eval_jaxpr/tkgs,skd->tkgd/dot_general | solution.py:24
  185.9 5.8 %fusion.85 = (f32[512,8]{0,1:T(8,128)S(1)}, f32[512,512,8]{1,0,2:T(8,128)}) fusion(pred[512,512]{0,1:T(8,128)(4,1)S(1)} %compare_and_fusion.2, bf16[512,1,8,128]{3,0,2,1:T(8,128)(2,1)S(1)} %get-tuple-element.569, bf16[4096,128]{1,0:T(8,128)(2,1)} %get-tuple-element.568, s32[]{:T(128)S(6)} %select_n.145), kind=kOutput, calls=%fused_computation.28.clone.1 | convolution fusion | flops 543158272 | bytes 9846788 | tf_op jit(solution)/shard_map/while/body/eval_jaxpr/tkgd,skd->tkgs/dot_general | solution.py:45
  191.7 4.6 %fusion.87 = f32[512,8]{0,1:T(8,128)S(1)} fusion(f32[512,512,8]{1,0,2:T(8,128)} %get-tuple-element.538, f32[512,8]{0,1:T(8,128)S(1)} %bitcast.195, pred[512,512]{0,1:T(8,128)(4,1)S(1)} %compare_and_fusion.2), kind=kLoop, calls=%fused_computation.30.clone.1 | loop fusion | flops 10481664 | bytes 8683520 | tf_op jit(solution)/shard_map/while/body/eval_jaxpr/reduce_sum | solution.py:23
  197.5 3.7 %bitcast_add_fusion.9 = f32[512,1,8,128]{0,3,2,1:T(8,128)S(1)} fusion(f32[512,1,8,128]{0,3,2,1:T(8,128)S(1)} %copy-done.2, f32[512,512,8]{1,0,2:T(8,128)S(1)} %copy-done.1, f32[512,8]{0,1:T(8,128)S(1)} %bitcast.196, pred[512,512]{0,1:T(8,128)(4,1)S(1)} %compare_and_fusion.2, f32[512,8]{0,1:T(8,128)S(1)} %get-tuple-element.539, pred[]{:T(512)S(6)} %compare.7, ...), kind=kOutput, calls=%fused_computation.34.clone.1 | convolution fusion | flops 548929536 | bytes 13008901 | tf_op jit(solution)/shard_map/while/body/eval_jaxpr/tkgs,skd->tkgd/dot_general | solution.py:24
  202.8 5.8 %fusion.85 = (f32[512,8]{0,1:T(8,128)S(1)}, f32[512,512,8]{1,0,2:T(8,128)}) fusion(pred[512,512]{0,1:T(8,128)(4,1)S(1)} %compare_and_fusion.2, bf16[512,1,8,128]{3,0,2,1:T(8,128)(2,1)S(1)} %get-tuple-element.569, bf16[4096,128]{1,0:T(8,128)(2,1)} %get-tuple-element.568, s32[]{:T(128)S(6)} %select_n.145), kind=kOutput, calls=%fused_computation.28.clone.1 | convolution fusion | flops 543158272 | bytes 9846788 | tf_op jit(solution)/shard_map/while/body/eval_jaxpr/tkgd,skd->tkgs/dot_general | solution.py:45
  208.6 4.6 %fusion.87 = f32[512,8]{0,1:T(8,128)S(1)} fusion(f32[512,512,8]{1,0,2:T(8,128)} %get-tuple-element.538, f32[512,8]{0,1:T(8,128)S(1)} %bitcast.195, pred[512,512]{0,1:T(8,128)(4,1)S(1)} %compare_and_fusion.2), kind=kLoop, calls=%fused_computation.30.clone.1 | loop fusion | flops 10481664 | bytes 8683520 | tf_op jit(solution)/shard_map/while/body/eval_jaxpr/reduce_sum | solution.py:23
  214.5 3.7 %bitcast_add_fusion.9 = f32[512,1,8,128]{0,3,2,1:T(8,128)S(1)} fusion(f32[512,1,8,128]{0,3,2,1:T(8,128)S(1)} %copy-done.2, f32[512,512,8]{1,0,2:T(8,128)S(1)} %copy-done.1, f32[512,8]{0,1:T(8,128)S(1)} %bitcast.196, pred[512,512]{0,1:T(8,128)(4,1)S(1)} %compare_and_fusion.2, f32[512,8]{0,1:T(8,128)S(1)} %get-tuple-element.539, pred[]{:T(512)S(6)} %compare.7, ...), kind=kOutput, calls=%fused_computation.34.clone.1 | convolution fusion | flops 548929536 | bytes 13008901 | tf_op jit(solution)/shard_map/while/body/eval_jaxpr/tkgs,skd->tkgd/dot_general | solution.py:24
  219.8 5.8 %fusion.85 = (f32[512,8]{0,1:T(8,128)S(1)}, f32[512,512,8]{1,0,2:T(8,128)}) fusion(pred[512,512]{0,1:T(8,128)(4,1)S(1)} %compare_and_fusion.2, bf16[512,1,8,128]{3,0,2,1:T(8,128)(2,1)S(1)} %get-tuple-element.569, bf16[4096,128]{1,0:T(8,128)(2,1)} %get-tuple-element.568, s32[]{:T(128)S(6)} %select_n.145), kind=kOutput, calls=%fused_computation.28.clone.1 | convolution fusion | flops 543158272 | bytes 9846788 | tf_op jit(solution)/shard_map/while/body/eval_jaxpr/tkgd,skd->tkgs/dot_general | solution.py:45
  225.6 4.6 %fusion.87 = f32[512,8]{0,1:T(8,128)S(1)} fusion(f32[512,512,8]{1,0,2:T(8,128)} %get-tuple-element.538, f32[512,8]{0,1:T(8,128)S(1)} %bitcast.195, pred[512,512]{0,1:T(8,128)(4,1)S(1)} %compare_and_fusion.2), kind=kLoop, calls=%fused_computation.30.clone.1 | loop fusion | flops 10481664 | bytes 8683520 | tf_op jit(solution)/shard_map/while/body/eval_jaxpr/reduce_sum | solution.py:23
  231.4 3.7 %bitcast_add_fusion.9 = f32[512,1,8,128]{0,3,2,1:T(8,128)S(1)} fusion(f32[512,1,8,128]{0,3,2,1:T(8,128)S(1)} %copy-done.2, f32[512,512,8]{1,0,2:T(8,128)S(1)} %copy-done.1, f32[512,8]{0,1:T(8,128)S(1)} %bitcast.196, pred[512,512]{0,1:T(8,128)(4,1)S(1)} %compare_and_fusion.2, f32[512,8]{0,1:T(8,128)S(1)} %get-tuple-element.539, pred[]{:T(512)S(6)} %compare.7, ...), kind=kOutput, calls=%fused_computation.34.clone.1 | convolution fusion | flops 548929536 | bytes 13008901 | tf_op jit(solution)/shard_map/while/body/eval_jaxpr/tkgs,skd->tkgd/dot_general | solution.py:24
  (281 shorter events, 94.9 us)
Async XLA Ops:
  7.2 20.3 %copy-start = (bf16[16,4,128]{2,1,0:T(4,128)(2,1)S(1)}, bf16[16,4,128]{2,1,0:T(4,128)(2,1)}, u32[]{:S(2)}) copy-start(bf16[16,4,128]{2,1,0:T(4,128)(2,1)} %param.23) | copy-start | bytes 49156
  7.2 93.7 %all-gather.3.cloned.1.call-start = ((), (), s32[]{:S(2)}) async-start(), calls=%async_computation.1 | async-start | bytes 1179648 | tf_op jit(solution)/shard_map/all_gather | solution.py:87
  11.0 12.1 %copy-start.5 = (bf16[1,512,128]{2,1,0:T(8,128)(2,1)S(1)}, bf16[1,512,128]{2,1,0:T(8,128)(2,1)}, u32[]{:S(2)}) copy-start(bf16[1,512,128]{2,1,0:T(8,128)(2,1)} %param.17) | copy-start | bytes 393220
  11.0 12.9 %copy-start.6 = (bf16[16,4,1024]{2,1,0:T(4,128)(2,1)S(1)}, bf16[16,4,1024]{2,1,0:T(4,128)(2,1)}, u32[]{:S(2)}) copy-start(bf16[16,4,1024]{2,1,0:T(4,128)(2,1)} %param.21) | copy-start | bytes 393220
  11.2 12.9 %copy-start.11 = (bf16[16,4,128]{2,1,0:T(4,128)(2,1)S(1)}, bf16[16,4,128]{2,1,0:T(4,128)(2,1)}, u32[]{:S(2)}) copy-start(bf16[16,4,128]{2,1,0:T(4,128)(2,1)} %param.22) | copy-start | bytes 49156
  15.8 17.0 %all-to-all-start = ((bf16[32,2,4096]{2,1,0:T(2,128)(2,1)}), bf16[32,2,4096]{2,1,0:T(2,128)(2,1)S(1)}, u32[]{:S(2)}, u32[]{:S(2)}) async-start(bf16[32,2,4096]{2,1,0:T(2,128)(2,1)} %reshape.362), calls=%async_computation | async-start | bytes 1048576 | tf_op jit(solution)/shard_map/all_to_all | solution.py:116
  23.1 77.8 %all-gather.5.cloned.1.call-start = ((), (), s32[]{:S(2)}) async-start(), calls=%async_computation.2 | async-start | bytes 1179648 | tf_op jit(solution)/shard_map/all_gather | solution.py:88
  38.1 3.6 %copy-start.9 = (s32[16,64]{1,0:T(8,128)S(1)}, s32[16,64]{1,0:T(8,128)}, u32[]{:S(2)}) copy-start(s32[16,64]{1,0:T(8,128)} %param.24) | copy-start | bytes 12292
  38.1 3.6 %copy-start.10 = (s32[16]{0:T(128)S(1)}, s32[16]{0:T(128)}, u32[]{:S(2)}) copy-start(s32[16]{0:T(128)} %param.25) | copy-start | bytes 196
  44.4 3.4 %copy-start.7 = (f32[16,4,1,8,128]{4,3,1,0,2:T(8,128)S(1)}, f32[16,4,1,8,128]{4,3,1,0,2:T(8,128)}, u32[]{:S(2)}) copy-start(f32[16,4,1,8,128]{4,3,1,0,2:T(8,128)} %get-tuple-element.593) | copy-start | bytes 786436 | tf_op jit(solution)/shard_map/while
  51.6 3.4 %copy-start.7 = (f32[16,4,1,8,128]{4,3,1,0,2:T(8,128)S(1)}, f32[16,4,1,8,128]{4,3,1,0,2:T(8,128)}, u32[]{:S(2)}) copy-start(f32[16,4,1,8,128]{4,3,1,0,2:T(8,128)} %get-tuple-element.593) | copy-start | bytes 786436 | tf_op jit(solution)/shard_map/while
  58.8 3.4 %copy-start.7 = (f32[16,4,1,8,128]{4,3,1,0,2:T(8,128)S(1)}, f32[16,4,1,8,128]{4,3,1,0,2:T(8,128)}, u32[]{:S(2)}) copy-start(f32[16,4,1,8,128]{4,3,1,0,2:T(8,128)} %get-tuple-element.593) | copy-start | bytes 786436 | tf_op jit(solution)/shard_map/while
  66.0 3.4 %copy-start.7 = (f32[16,4,1,8,128]{4,3,1,0,2:T(8,128)S(1)}, f32[16,4,1,8,128]{4,3,1,0,2:T(8,128)}, u32[]{:S(2)}) copy-start(f32[16,4,1,8,128]{4,3,1,0,2:T(8,128)} %get-tuple-element.593) | copy-start | bytes 786436 | tf_op jit(solution)/shard_map/while
  73.2 3.4 %copy-start.7 = (f32[16,4,1,8,128]{4,3,1,0,2:T(8,128)S(1)}, f32[16,4,1,8,128]{4,3,1,0,2:T(8,128)}, u32[]{:S(2)}) copy-start(f32[16,4,1,8,128]{4,3,1,0,2:T(8,128)} %get-tuple-element.593) | copy-start | bytes 786436 | tf_op jit(solution)/shard_map/while
  87.5 3.4 %copy-start.7 = (f32[16,4,1,8,128]{4,3,1,0,2:T(8,128)S(1)}, f32[16,4,1,8,128]{4,3,1,0,2:T(8,128)}, u32[]{:S(2)}) copy-start(f32[16,4,1,8,128]{4,3,1,0,2:T(8,128)} %get-tuple-element.593) | copy-start | bytes 786436 | tf_op jit(solution)/shard_map/while
  94.6 3.4 %copy-start.7 = (f32[16,4,1,8,128]{4,3,1,0,2:T(8,128)S(1)}, f32[16,4,1,8,128]{4,3,1,0,2:T(8,128)}, u32[]{:S(2)}) copy-start(f32[16,4,1,8,128]{4,3,1,0,2:T(8,128)} %get-tuple-element.593) | copy-start | bytes 786436 | tf_op jit(solution)/shard_map/while
  101.1 10.4 %copy-start.2 = (f32[512,1,8,128]{0,3,2,1:T(8,128)S(1)}, f32[512,1,8,128]{0,3,2,1:T(8,128)}, u32[]{:S(2)}) copy-start(f32[512,1,8,128]{0,3,2,1:T(8,128)} %get-tuple-element.555) | copy-start | bytes 6291460 | tf_op jit(solution)/shard_map/while
  106.9 5.8 %copy-start.1 = (f32[512,512,8]{1,0,2:T(8,128)S(1)}, f32[512,512,8]{1,0,2:T(8,128)}, u32[]{:S(2)}) copy-start(f32[512,512,8]{1,0,2:T(8,128)} %get-tuple-element.538) | copy-start | bytes 25165828 | tf_op jit(solution)/shard_map/while
  118.1 10.4 %copy-start.2 = (f32[512,1,8,128]{0,3,2,1:T(8,128)S(1)}, f32[512,1,8,128]{0,3,2,1:T(8,128)}, u32[]{:S(2)}) copy-start(f32[512,1,8,128]{0,3,2,1:T(8,128)} %get-tuple-element.555) | copy-start | bytes 6291460 | tf_op jit(solution)/shard_map/while
  123.9 5.8 %copy-start.1 = (f32[512,512,8]{1,0,2:T(8,128)S(1)}, f32[512,512,8]{1,0,2:T(8,128)}, u32[]{:S(2)}) copy-start(f32[512,512,8]{1,0,2:T(8,128)} %get-tuple-element.538) | copy-start | bytes 25165828 | tf_op jit(solution)/shard_map/while
  135.0 10.4 %copy-start.2 = (f32[512,1,8,128]{0,3,2,1:T(8,128)S(1)}, f32[512,1,8,128]{0,3,2,1:T(8,128)}, u32[]{:S(2)}) copy-start(f32[512,1,8,128]{0,3,2,1:T(8,128)} %get-tuple-element.555) | copy-start | bytes 6291460 | tf_op jit(solution)/shard_map/while
  140.8 5.8 %copy-start.1 = (f32[512,512,8]{1,0,2:T(8,128)S(1)}, f32[512,512,8]{1,0,2:T(8,128)}, u32[]{:S(2)}) copy-start(f32[512,512,8]{1,0,2:T(8,128)} %get-tuple-element.538) | copy-start | bytes 25165828 | tf_op jit(solution)/shard_map/while
  152.0 10.4 %copy-start.2 = (f32[512,1,8,128]{0,3,2,1:T(8,128)S(1)}, f32[512,1,8,128]{0,3,2,1:T(8,128)}, u32[]{:S(2)}) copy-start(f32[512,1,8,128]{0,3,2,1:T(8,128)} %get-tuple-element.555) | copy-start | bytes 6291460 | tf_op jit(solution)/shard_map/while
  157.8 5.8 %copy-start.1 = (f32[512,512,8]{1,0,2:T(8,128)S(1)}, f32[512,512,8]{1,0,2:T(8,128)}, u32[]{:S(2)}) copy-start(f32[512,512,8]{1,0,2:T(8,128)} %get-tuple-element.538) | copy-start | bytes 25165828 | tf_op jit(solution)/shard_map/while
  168.9 10.4 %copy-start.2 = (f32[512,1,8,128]{0,3,2,1:T(8,128)S(1)}, f32[512,1,8,128]{0,3,2,1:T(8,128)}, u32[]{:S(2)}) copy-start(f32[512,1,8,128]{0,3,2,1:T(8,128)} %get-tuple-element.555) | copy-start | bytes 6291460 | tf_op jit(solution)/shard_map/while
  174.7 5.8 %copy-start.1 = (f32[512,512,8]{1,0,2:T(8,128)S(1)}, f32[512,512,8]{1,0,2:T(8,128)}, u32[]{:S(2)}) copy-start(f32[512,512,8]{1,0,2:T(8,128)} %get-tuple-element.538) | copy-start | bytes 25165828 | tf_op jit(solution)/shard_map/while
  185.9 10.4 %copy-start.2 = (f32[512,1,8,128]{0,3,2,1:T(8,128)S(1)}, f32[512,1,8,128]{0,3,2,1:T(8,128)}, u32[]{:S(2)}) copy-start(f32[512,1,8,128]{0,3,2,1:T(8,128)} %get-tuple-element.555) | copy-start | bytes 6291460 | tf_op jit(solution)/shard_map/while
  191.7 5.8 %copy-start.1 = (f32[512,512,8]{1,0,2:T(8,128)S(1)}, f32[512,512,8]{1,0,2:T(8,128)}, u32[]{:S(2)}) copy-start(f32[512,512,8]{1,0,2:T(8,128)} %get-tuple-element.538) | copy-start | bytes 25165828 | tf_op jit(solution)/shard_map/while
  202.8 10.4 %copy-start.2 = (f32[512,1,8,128]{0,3,2,1:T(8,128)S(1)}, f32[512,1,8,128]{0,3,2,1:T(8,128)}, u32[]{:S(2)}) copy-start(f32[512,1,8,128]{0,3,2,1:T(8,128)} %get-tuple-element.555) | copy-start | bytes 6291460 | tf_op jit(solution)/shard_map/while
  208.6 5.8 %copy-start.1 = (f32[512,512,8]{1,0,2:T(8,128)S(1)}, f32[512,512,8]{1,0,2:T(8,128)}, u32[]{:S(2)}) copy-start(f32[512,512,8]{1,0,2:T(8,128)} %get-tuple-element.538) | copy-start | bytes 25165828 | tf_op jit(solution)/shard_map/while
  219.8 10.4 %copy-start.2 = (f32[512,1,8,128]{0,3,2,1:T(8,128)S(1)}, f32[512,1,8,128]{0,3,2,1:T(8,128)}, u32[]{:S(2)}) copy-start(f32[512,1,8,128]{0,3,2,1:T(8,128)} %get-tuple-element.555) | copy-start | bytes 6291460 | tf_op jit(solution)/shard_map/while
  225.6 5.8 %copy-start.1 = (f32[512,512,8]{1,0,2:T(8,128)S(1)}, f32[512,512,8]{1,0,2:T(8,128)}, u32[]{:S(2)}) copy-start(f32[512,512,8]{1,0,2:T(8,128)} %get-tuple-element.538) | copy-start | bytes 25165828 | tf_op jit(solution)/shard_map/while
  (18 other events, 21.5 us)
Sparse Core Ops, SparseCore 0:
  9.9 29.5 all-gather.2
  41.3 27.5 all-gather.4
where the time goes:
time: 251 us; the launch traced here: 246 us
  matrix products  85.5 us (34%)
  local copies, waits for them, and re-layouts  77.2 us (31%)
  other arithmetic  55.9 us (22%)
  between operations  14.3 us (6%)
  starting transfers between devices  7.39 us (3%)
  waiting for transfers between devices  4.99 us (2%)
    dot_general x8, matrix products, span_advance(): jnp.einsum('tkgd,skd->tkgs', query, key_block, preferred_element_type=jnp...  46 us
    reduce_sum x17, other arithmetic, online_update(): total = total * factor + jnp.sum(weights, axis=-1)  39.5 us
    dot_general x17, matrix products, online_update(): jnp.einsum(pattern, weights.astype(jnp.bfloat16), values_block, preferred...  33.5 us
    while x96, local copies, waits for them, and re-layouts  25.8 us
    gather x8, local copies, waits for them, and re-layouts, body_advance(): key_block = all_keys[entries].reshape(requests, window, kv_local, HEAD_DIM)  19.5 us
    gather x8, local copies, waits for them, and re-layouts, body_advance(): all_values[entries].reshape(requests, window, kv_local, HEAD_DIM)  19.5 us
    all_to_all x1, starting transfers between devices, on_device(): lax.all_to_all(outgoing, ('section', 'seq'), split_axis=0, concat_axis=0,...  7.31 us
    unnamed x21, local copies, waits for them, and re-layouts  6.54 us
  transfers between devices with their start and end apart: 3, of which 1 were waited for; matrix products, arithmetic and copies ran while one was open for 30% of the time, Pallas kernels for 0%

commit v1 on v0

v1 whole, which is shorter than its diff:
```python
import functools
import math

import jax
import jax.numpy as jnp
from jax import lax
from jax.experimental import pallas as pl
from jax.experimental.pallas import tpu as pltpu
from jax.sharding import PartitionSpec as P

MESH = pl.DeviceIdType.MESH
HD = 128
PAGE = 32
MAXPG = 64
STEPS = 4
GROUP = 8
TOK = 512
VROWS = 144
POOL = 256
REQS = 16
CTX = MAXPG * PAGE
ROWS = STEPS * GROUP
SCALE = math.log2(math.e) / math.sqrt(HD)
LIMIT = 2.0**100
LOW = -1e30
NT = (((1,), (1,)), ((), ()))


def dot_nt(a, b):
    return lax.dot_general(a, b, NT, preferred_element_type=jnp.float32)


def dot_nn(a, b):
    return jnp.dot(a, b, preferred_element_type=jnp.float32)


def prefill_kernel(
    chips, sections,
    q_ref, k_ref, v_ref, owner_ref,
    out_ref, total_ref, karch_ref, varch_ref, arrived_ref,
    kall, vall, acc, shift, pages,
    ksend, vsend, krecv, vrecv, fksend, fvsend, psend, precv, asem,
):
    section = lax.axis_index("section")
    seq = lax.axis_index("seq")
    tensor = lax.axis_index("tensor")
    width = 2 * chips
    count = sections * width
    chip, core = seq // 2, seq % 2
    mate = chip * 2 + (1 - core)
    block = section * width + seq

    barrier = pltpu.get_barrier_semaphore()

    @pl.loop(1, count)
    def _(step):
        other = lax.rem(block + step, count)
        pl.semaphore_signal(
            barrier, inc=1,
            device_id=(other // width, lax.rem(other, width), tensor), device_id_type=MESH,
        )

    own_k = k_ref[...].reshape(TOK, HD)
    own_v = v_ref[...].reshape(TOK, HD)
    vall[seq, :HD, :] = own_v.T
    for index in range(width):
        vall[index, HD:, :] = jnp.ones((VROWS - HD, TOK), jnp.bfloat16)
    pl.semaphore_wait(barrier, count - 1)

    def k_copy(source, held, target, ssem):
        return pltpu.make_async_remote_copy(
            src_ref=source, dst_ref=kall.at[held], send_sem=ssem, recv_sem=krecv.at[held],
            device_id=(section, target, tensor), device_id_type=MESH,
        )

    def v_copy(held, target, ssem):
        return pltpu.make_async_remote_copy(
            src_ref=vall.at[held, pl.ds(0, HD)], dst_ref=vall.at[held, pl.ds(0, HD)],
            send_sem=ssem, recv_sem=vrecv.at[held],
            device_id=(section, target, tensor), device_id_type=MESH,
        )

    @pl.when(core == 0)
    def _():
        k_copy(k_ref, seq, mate, fksend.at[chip]).start()
        v_copy(seq, mate, fvsend.at[chip]).start()

    @pl.loop(chip + 1, chips)
    def _(far):
        target = far * 2 + core
        k_copy(k_ref, seq, target, ksend.at[far]).start()
        v_copy(seq, target, vsend.at[far]).start()

    def page_copy(step):
        other = lax.rem(block + step, count)
        return pltpu.make_async_remote_copy(
            src_ref=pages.at[other], dst_ref=arrived_ref.at[block],
            send_sem=psend.at[other], recv_sem=precv.at[block],
            device_id=(other // width, lax.rem(other, width), tensor), device_id_type=MESH,
        )

    def fill_page(target):
        place = jnp.int32(0)
        for page in range(TOK // PAGE):
            place = jnp.where(owner_ref[0, page] == target, page, place)
        pages[target, :PAGE, :] = k_ref[place]
        pages[target, PAGE:, :] = v_ref[place]

    fill_page(block)
    own_page = pltpu.make_async_copy(pages.at[block], arrived_ref.at[block], asem.at[0])
    own_page.start()

    @pl.loop(1, count)
    def _(step):
        fill_page(lax.rem(block + step, count))
        page_copy(step).start()

    ones = jnp.ones((8, HD), jnp.bfloat16)
    half = TOK // 2
    k_low, k_high = own_k[:half], own_k[half:]
    key_at = lax.broadcasted_iota(jnp.int32, (half, TOK), 0)
    query_at = lax.broadcasted_iota(jnp.int32, (half, TOK), 1)
    low_valid = key_at <= query_at
    high_valid = low_valid[:, :half]

    def query(head):
        return q_ref[0, :, head * HD:(head + 1) * HD]

    shifts = []
    for head in range(GROUP):
        product = (query(head).astype(jnp.float32) * own_k.astype(jnp.float32)).astype(jnp.bfloat16)
        shifts.append(dot_nt(ones, product)[:1])
    for head in range(GROUP):
        shift[head] = shifts[head]

    def own_scores(head):
        q = query(head)
        return dot_nt(k_low, q), dot_nt(k_high, q[half:])

    scores = own_scores(0)
    for head in range(GROUP):
        following = own_scores(head + 1) if head + 1 < GROUP else None
        base = shift[head]
        low = jnp.where(low_valid, jnp.exp2((scores[0] - base) * SCALE), 0.0)
        high = jnp.where(high_valid, jnp.exp2((scores[1] - base[:, half:]) * SCALE), 0.0)
        first = dot_nn(vall[seq, :, :half], low.astype(jnp.bfloat16))
        second = dot_nn(vall[seq, :, half:], high.astype(jnp.bfloat16))
        acc[head, :, :half] = first[:, :half]
        acc[head, :, half:] = first[:, half:] + second
        scores = following

    def attend(held_blocks):
        keys = jnp.concatenate([kall[b].reshape(TOK, HD) for b in held_blocks], axis=0)
        values = jnp.concatenate([vall[b] for b in held_blocks], axis=1)
        scores = dot_nt(keys, query(0))
        for head in range(GROUP):
            following = dot_nt(keys, query(head + 1)) if head + 1 < GROUP else None
            weights = jnp.exp2((scores - shift[head]) * SCALE).astype(jnp.bfloat16)
            acc[head] += dot_nn(values, weights)
            scores = following

    def archive(held):
        return (
            pltpu.make_async_copy(kall.at[held], karch_ref.at[held], asem.at[1 + 2 * held]),
            pltpu.make_async_copy(vall.at[held], varch_ref.at[held], asem.at[2 + 2 * held]),
        )

    kall[seq] = k_ref[...]
    for copy in archive(seq):
        copy.start()

    @pl.when(core == 1)
    def _():
        k_copy(k_ref, mate, seq, fksend.at[0]).wait_recv()
        v_copy(mate, seq, fvsend.at[0]).wait_recv()
        for copy in archive(mate):
            copy.start()
        attend([mate])

    def near_first(step):
        if chips == 4:
            order = jnp.where(chip == 3, jnp.where(step == 0, 2, jnp.where(step == 1, 0, 1)), chip - 1 - step)
        else:
            order = chip - 1 - step
        return order

    @pl.loop(0, chip)
    def _(step):
        far = near_first(step)
        direct = far * 2 + core
        passed = far * 2 + 1 - core
        k_copy(k_ref, direct, seq, ksend.at[0]).wait_recv()
        k_copy(kall.at[direct], direct, mate, fksend.at[far]).start()
        v_copy(direct, seq, vsend.at[0]).wait_recv()
        v_copy(direct, mate, fvsend.at[far]).start()
        for copy in archive(direct):
            copy.start()
        k_copy(k_ref, passed, seq, ksend.at[0]).wait_recv()
        v_copy(passed, seq, vsend.at[0]).wait_recv()
        for copy in archive(passed):
            copy.start()
        attend([direct, passed])

    for head in range(GROUP):
        state = acc[head]
        total = state[HD:HD + 1]
        total_ref[head:head + 1, :] = total
        out_ref[0, :, head * HD:(head + 1) * HD] = (state[:HD] / total).astype(jnp.bfloat16).T

    for copy in archive(seq):
        copy.wait()

    @pl.when(core == 1)
    def _():
        for copy in archive(mate):
            copy.wait()

    @pl.loop(0, chip)
    def _(far):
        for held in (far * 2, far * 2 + 1):
            for copy in archive(held):
                copy.wait()
        k_copy(k_ref, seq, mate, fksend.at[far]).wait_send()
        v_copy(seq, mate, fvsend.at[far]).wait_send()

    @pl.when(core == 0)
    def _():
        k_copy(k_ref, seq, mate, fksend.at[chip]).wait_send()
        v_copy(seq, mate, fvsend.at[chip]).wait_send()

    @pl.loop(chip + 1, chips)
    def _(far):
        k_copy(k_ref, seq, mate, ksend.at[far]).wait_send()
        v_copy(seq, mate, vsend.at[far]).wait_send()

    own_page.wait()

    @pl.loop(1, count)
    def _(step):
        other = lax.rem(block + step, count)
        page_copy(step).wait_send()
        pltpu.make_async_remote_copy(
            src_ref=pages.at[other], dst_ref=arrived_ref.at[other],
            send_sem=psend.at[other], recv_sem=precv.at[other],
            device_id=(section, seq, tensor), device_id_type=MESH,
        ).wait_recv()


def decode_kernel(
    count, gang,
    table_ref, length_ref,
    sq_ref, sk_ref, sv_ref, poolk_ref, poolv_ref, arrived_ref, early_ref, total_ref,
    q_ref, karch_ref, varch_ref,
    final_ref, out_ref,
    kpages, vpages, q_all, new_part, sems,
    q_slow, k_slow, v_slow, o_slow,
):
    copies = [pltpu.make_async_copy(early_ref, final_ref, sems.at[0])]
    pieces = 4
    size = POOL // pieces
    loads = []
    for i in range(pieces):
        span = pl.ds(i * size, size)
        loads.append(pltpu.make_async_copy(poolk_ref.at[span], kpages.at[span], sems.at[1 + 2 * i]))
        loads.append(pltpu.make_async_copy(poolv_ref.at[span], vpages.at[span], sems.at[2 + 2 * i]))
    place = pl.ds(POOL, count)
    loads.append(pltpu.make_async_copy(arrived_ref.at[:, pl.ds(0, PAGE)], kpages.at[place], sems.at[9]))
    loads.append(pltpu.make_async_copy(arrived_ref.at[:, pl.ds(PAGE, PAGE)], vpages.at[place], sems.at[10]))
    for copy in loads + copies:
        copy.start()

    for r in range(REQS):
        wide = sq_ref[r].astype(jnp.float32)
        q_all[r] = jnp.concatenate(
            [wide[:, h * HD:(h + 1) * HD] for h in range(GROUP)], axis=0
        ).astype(jnp.bfloat16)
    new_k = jnp.concatenate([sk_ref[r].astype(jnp.float32) for r in range(REQS)], 0).astype(jnp.bfloat16)
    new_v = jnp.concatenate([sv_ref[r].astype(jnp.float32) for r in range(REQS)], 0).astype(jnp.bfloat16)
    new_scores = dot_nt(q_all[...].reshape(REQS * ROWS, HD), new_k)
    shape = (REQS * ROWS, REQS * STEPS)
    row = lax.broadcasted_iota(jnp.int32, shape, 0)
    column = lax.broadcasted_iota(jnp.int32, shape, 1)
    fits = (column // STEPS == row // ROWS) & (column % STEPS <= row % STEPS)
    new_part[...] = jnp.where(fits, new_scores, LOW).reshape(REQS, ROWS, REQS * STEPS)

    for copy in loads:
        copy.wait()

    position = lax.broadcasted_iota(jnp.int32, (ROWS, CTX), 1)
    cut = 8

    @pl.loop(0, REQS // gang)
    def _(turn):
        scores, extras = [], []
        for g in range(gang):
            r = turn * gang + g
            q = q_all[r]
            parts = []
            for b in range(MAXPG // cut):
                keys = jnp.concatenate([kpages[table_ref[r, b * cut + i]] for i in range(cut)], axis=0)
                parts.append(dot_nt(q, keys))
            scores.append(jnp.where(position < length_ref[r], jnp.concatenate(parts, axis=1), LOW))
            extras.append(new_part[r])
        for g in range(gang):
            r = turn * gang + g
            top = jnp.maximum(
                jnp.max(scores[g], axis=1, keepdims=True), jnp.max(extras[g], axis=1, keepdims=True)
            )
            weights = jnp.exp2((scores[g] - top) * SCALE)
            extra = jnp.exp2((extras[g] - top) * SCALE)
            total = jnp.sum(weights, axis=1, keepdims=True) + jnp.sum(extra, axis=1, keepdims=True)
            weights = weights.astype(jnp.bfloat16)
            summed = dot_nn(extra.astype(jnp.bfloat16), new_v)
            for b in range(MAXPG // cut):
                values = jnp.concatenate([vpages[table_ref[r, b * cut + i]] for i in range(cut)], axis=0)
                summed += dot_nn(weights[:, b * cut * PAGE:(b + 1) * cut * PAGE], values)
            result = summed / total
            out_ref[r] = jnp.concatenate(
                [result[h * STEPS:(h + 1) * STEPS] for h in range(GROUP)], axis=1
            ).astype(jnp.bfloat16)

    for copy in copies:
        copy.wait()

    fine = jnp.min(jnp.where(total_ref[...] < LIMIT, 1.0, 0.0)) > 0.5

    @pl.when(jnp.logical_not(fine))
    def _():
        seq = lax.axis_index("seq")
        load = pltpu.make_async_copy(q_ref, q_slow, sems.at[0])
        load.start()
        load.wait()
        key_at = lax.broadcasted_iota(jnp.int32, (TOK, TOK), 0)
        query_at = lax.broadcasted_iota(jnp.int32, (TOK, TOK), 1)
        for head in range(GROUP):
            q = q_slow[0, :, head * HD:(head + 1) * HD]

            def advance(held, state):
                top, state_acc = state
                loads = (
                    pltpu.make_async_copy(karch_ref.at[held], k_slow, sems.at[1]),
                    pltpu.make_async_copy(varch_ref.at[held], v_slow, sems.at[2]),
                )
                for copy in loads:
                    copy.start()
                for copy in loads:
                    copy.wait()
                valid = key_at + held * TOK <= query_at + seq * TOK
                s = jnp.where(valid, dot_nt(k_slow[...].reshape(TOK, HD), q), LOW)
                fresh = jnp.maximum(top, jnp.max(s, axis=0, keepdims=True))
                w = jnp.exp2((s - fresh) * SCALE).astype(jnp.bfloat16)
                return fresh, state_acc * jnp.exp2((top - fresh) * SCALE) + dot_nn(v_slow[...], w)

            start = (jnp.full((1, TOK), LOW, jnp.float32), jnp.zeros((VROWS, TOK), jnp.float32))
            _, state = lax.fori_loop(0, seq + 1, lambda i, s: advance(seq - i, s), start)
            o_slow[0, :, head * HD:(head + 1) * HD] = (state[:HD] / state[HD:HD + 1]).astype(jnp.bfloat16).T
        store = pltpu.make_async_copy(o_slow, final_ref, sems.at[0])
        store.start()
        store.wait()


def on_device(
    prompt_query, prompt_keys, prompt_values, page_owner, pool_keys, pool_values,
    step_query, step_keys, step_values, page_table, context_len,
):
    sections = lax.axis_size("section")
    width = lax.axis_size("seq")
    count = sections * width
    chips = width // 2
    bf16, f32 = jnp.bfloat16, jnp.float32
    vmem = pl.BlockSpec(memory_space=pltpu.VMEM)
    smem = pl.BlockSpec(memory_space=pltpu.SMEM)
    hbm = pl.BlockSpec(memory_space=pl.ANY)
    pages = TOK // PAGE
    dma = pltpu.SemaphoreType.DMA
    early, totals, karch, varch, arrived = pl.pallas_call(
        functools.partial(prefill_kernel, chips, sections),
        out_shape=(
            jax.ShapeDtypeStruct((1, TOK, GROUP * HD), bf16),
            jax.ShapeDtypeStruct((GROUP, TOK), f32),
            jax.ShapeDtypeStruct((width, pages, PAGE, HD), bf16),
            jax.ShapeDtypeStruct((width, VROWS, TOK), bf16),
            jax.ShapeDtypeStruct((count, 2 * PAGE, HD), bf16),
        ),
        in_specs=[vmem, vmem, vmem, smem],
        out_specs=(vmem, vmem, hbm, hbm, hbm),
        scratch_shapes=[
            pltpu.VMEM((width, pages, PAGE, HD), bf16),
            pltpu.VMEM((width, VROWS, TOK), bf16),
            pltpu.VMEM((GROUP, VROWS, TOK), f32),
            pltpu.VMEM((GROUP, 1, TOK), f32),
            pltpu.VMEM((count, 2 * PAGE, HD), bf16),
            dma((chips,)), dma((chips,)), dma((width,)), dma((width,)),
            dma((chips,)), dma((chips,)), dma((count,)), dma((count,)),
            dma((1 + 2 * width,)),
        ],
        compiler_params=pltpu.CompilerParams(
            collective_id=0, has_side_effects=True, vmem_limit_bytes=32 * 2**20
        ),
        name="prefill",
    )(
        prompt_query,
        prompt_keys.reshape(pages, PAGE, HD),
        prompt_values.reshape(pages, PAGE, HD),
        page_owner,
    )
    return pl.pallas_call(
        functools.partial(decode_kernel, count, 4),
        out_shape=(
            jax.ShapeDtypeStruct((1, TOK, GROUP * HD), bf16),
            jax.ShapeDtypeStruct((REQS, STEPS, GROUP * HD), bf16),
        ),
        in_specs=[smem, smem, vmem, vmem, vmem, hbm, hbm, hbm, hbm, vmem, hbm, hbm, hbm],
        out_specs=(hbm, vmem),
        scratch_shapes=[
            pltpu.VMEM((POOL + count, PAGE, HD), bf16),
            pltpu.VMEM((POOL + count, PAGE, HD), bf16),
            pltpu.VMEM((REQS, ROWS, HD), bf16),
            pltpu.VMEM((REQS, ROWS, REQS * STEPS), f32),
            dma((11,)),
            pltpu.VMEM((1, TOK, GROUP * HD), bf16),
            pltpu.VMEM((pages, PAGE, HD), bf16),
            pltpu.VMEM((VROWS, TOK), bf16),
            pltpu.VMEM((1, TOK, GROUP * HD), bf16),
        ],
        compiler_params=pltpu.CompilerParams(vmem_limit_bytes=32 * 2**20),
        name="decode",
    )(
        page_table, context_len, step_query, step_keys, step_values, pool_keys, pool_values,
        arrived, early, totals, prompt_query, karch, varch,
    )


def solution(mesh):
    in_specs = (
        P("section", "seq", "tensor"),
        P("section", "seq", "tensor"),
        P("section", "seq", "tensor"),
        P("section", "seq"),
        P(("section", "seq"), None, "tensor"),
        P(("section", "seq"), None, "tensor"),
        P(("section", "seq"), None, "tensor"),
        P(("section", "seq"), None, "tensor"),
        P(("section", "seq"), None, "tensor"),
        P(("section", "seq"), None),
        P(("section", "seq")),
    )
    out_specs = (P("section", "seq", "tensor"), P(("section", "seq"), None, "tensor"))
    return jax.shard_map(
        on_device, mesh=mesh, in_specs=in_specs, out_specs=out_specs, check_vma=False
    )
```

time: 251 us -> 55.7 us (0.22); the launches traced: 246 us -> 55.3 us
  matrix products: 85.5 us -> 0 us
  local copies, waits for them, and re-layouts: 77.2 us -> 10.5 us
  other arithmetic: 55.9 us -> 0 us
  Pallas kernels: 0 us -> 43.9 us
  between operations: 14.3 us -> 0.85 us
  starting transfers between devices: 7.39 us -> 0 us
  waiting for transfers between devices: 4.99 us -> 0 us
    dot_general x35 -> x0, matrix products: 85.5 us -> none  [the longest x8 46 us: span_advance(): jnp.einsum('tkgd,skd->tkgs', query, key_block, preferred_element_type=jnp...]
    pallas_call x0 -> x2, Pallas kernels: none -> 43.9 us  [the longest x1 36.8 us: on_device(): pl.pallas_call(functools.partial(prefill_kernel, chips, sections), out_sh...]
    reduce_sum x18 -> x0, other arithmetic: 40.4 us -> none  [the longest x17 39.5 us: online_update(): total = total * factor + jnp.sum(weights, axis=-1)]
    gather x16 -> x0, local copies, waits for them, and re-layouts: 39 us -> none  [the longest x8 19.5 us: body_advance(): key_block = all_keys[entries].reshape(requests, window, kv_local, HEAD_DIM)]
    while x96 -> x0, local copies, waits for them, and re-layouts: 25.8 us -> none
    all_to_all x1 -> x0, starting transfers between devices: 7.31 us -> none  [on_device(): lax.all_to_all(outgoing, ('section', 'seq'), split_axis=0, concat_axis=0,...]
    all_to_all x1 -> x0, waiting for transfers between devices: 4.29 us -> none  [on_device(): lax.all_to_all(outgoing, ('section', 'seq'), split_axis=0, concat_axis=0,...]
    all_to_all x2 -> x0, other arithmetic: 4.18 us -> none  [on_device(): lax.all_to_all(outgoing, ('section', 'seq'), split_axis=0, concat_axis=0,...]
  transfers between devices with their start and end apart: 3 -> 0, of which waited for: 1 -> 0; matrix products, arithmetic and copies ran while one was open for 30% -> 0% of each run, Pallas kernels for 0% -> 0%
where the time goes in v1:
time: 55.7 us; the launch traced here: 55.3 us
  Pallas kernels  43.9 us (79%)
  local copies, waits for them, and re-layouts  10.5 us (19%)
  between operations  0.85 us (2%)
    pallas_call x1, Pallas kernels, on_device(): pl.pallas_call(functools.partial(prefill_kernel, chips, sections), out_sh...  36.8 us
    unnamed x22, local copies, waits for them, and re-layouts  10.5 us
    pallas_call x1, Pallas kernels, on_device(): pl.pallas_call(functools.partial(decode_kernel, count, 4), out_shape=(jax...  7.14 us

profile of v1, /device:TPU:120, one launch (start us, length us, event | category | flops | bytes accessed | tf_op | source)
XLA Modules:
  0.0 55.3 jit_solution(10424307434726319164)
XLA Ops:
  0.6 0.0 copy-start
  0.6 1.2 %copy-done = bf16[1,512,1024]{2,1,0:T(8,128)(2,1)S(1)} copy-done((bf16[1,512,1024]{2,1,0:T(8,128)(2,1)S(1)}, bf16[1,512,1024]{2,1,0:T(8,128)(2,1)}, u32[]{:S(2)}) %copy-start) | copy-done | bytes 1048600
  1.9 0.0 copy-start.4
  1.9 0.9 %copy-done.4 = bf16[1,512,128]{2,1,0:T(8,128)(2,1)S(1)} copy-done((bf16[1,512,128]{2,1,0:T(8,128)(2,1)S(1)}, bf16[1,512,128]{2,1,0:T(8,128)(2,1)}, u32[]{:S(2)}) %copy-start.4) | copy-done | bytes 131096
  2.8 0.0 copy-start.5
  2.8 0.9 %copy-done.5 = bf16[1,512,128]{2,1,0:T(8,128)(2,1)S(1)} copy-done((bf16[1,512,128]{2,1,0:T(8,128)(2,1)S(1)}, bf16[1,512,128]{2,1,0:T(8,128)(2,1)}, u32[]{:S(2)}) %copy-start.5) | copy-done | bytes 131096
  3.7 0.0 copy-start.9
  3.7 0.7 %copy-done.9 = s32[1,16]{1,0:T(1,128)S(1)} copy-done((s32[1,16]{1,0:T(1,128)S(1)}, s32[1,16]{1,0:T(1,128)}, u32[]{:S(2)}) %copy-start.9) | copy-done | bytes 88
  4.3 36.8 %prefill.1 = (bf16[1,512,1024]{2,1,0:T(8,128)(2,1)S(1)}, f32[8,512]{1,0:T(8,128)S(1)}, bf16[8,16,32,128]{3,2,1,0:T(8,128)(2,1)S(1)}, bf16[8,144,512]{2,1,0:T(8,128)(2,1)S(1)}, bf16[32,64,128]{2,1,0:T(8,128)(2,1)S(1)}) custom-call(bf16[1,512,1024]{2,1,0:T(8,128)(2,1)S(1)} %copy-done, bf16[16,32,128]{2,1,0:T(8,128)(2,1)S(1)} %bitcast.2, ...), custom_call_target="tpu_custom_call" | custom-call | tf_op jit(solution)/shard_map/prefill/pallas_call | solution.py:376
  41.1 0.0 copy-start.1
  41.1 1.6 %copy-done.1 = bf16[256,32,128]{2,1,0:T(8,128)(2,1)S(1)} copy-done((bf16[256,32,128]{2,1,0:T(8,128)(2,1)S(1)}, bf16[256,32,128]{2,1,0:T(8,128)(2,1)}, u32[]{:S(2)}) %copy-start.1) | copy-done | bytes 2097176
  42.7 0.0 copy-start.2
  42.7 1.6 %copy-done.2 = bf16[256,32,128]{2,1,0:T(8,128)(2,1)S(1)} copy-done((bf16[256,32,128]{2,1,0:T(8,128)(2,1)S(1)}, bf16[256,32,128]{2,1,0:T(8,128)(2,1)}, u32[]{:S(2)}) %copy-start.2) | copy-done | bytes 2097176
  44.3 0.0 copy-start.3
  44.3 0.9 %copy-done.3 = bf16[16,4,1024]{2,1,0:T(4,128)(2,1)S(1)} copy-done((bf16[16,4,1024]{2,1,0:T(4,128)(2,1)S(1)}, bf16[16,4,1024]{2,1,0:T(4,128)(2,1)}, u32[]{:S(2)}) %copy-start.3) | copy-done | bytes 131096
  45.2 0.0 copy-start.6
  45.2 0.7 %copy-done.6 = bf16[16,4,128]{2,1,0:T(4,128)(2,1)S(1)} copy-done((bf16[16,4,128]{2,1,0:T(4,128)(2,1)S(1)}, bf16[16,4,128]{2,1,0:T(4,128)(2,1)}, u32[]{:S(2)}) %copy-start.6) | copy-done | bytes 16408
  45.9 0.0 copy-start.7
  45.9 0.7 %copy-done.7 = bf16[16,4,128]{2,1,0:T(4,128)(2,1)S(1)} copy-done((bf16[16,4,128]{2,1,0:T(4,128)(2,1)S(1)}, bf16[16,4,128]{2,1,0:T(4,128)(2,1)}, u32[]{:S(2)}) %copy-start.7) | copy-done | bytes 16408
  46.6 0.0 copy-start.8
  46.6 0.7 %copy-done.8 = s32[16,64]{1,0:T(8,128)S(1)} copy-done((s32[16,64]{1,0:T(8,128)S(1)}, s32[16,64]{1,0:T(8,128)}, u32[]{:S(2)}) %copy-start.8) | copy-done | bytes 4120
  47.3 0.0 copy-start.10
  47.3 0.7 %copy-done.10 = s32[16]{0:T(128)S(1)} copy-done((s32[16]{0:T(128)S(1)}, s32[16]{0:T(128)}, u32[]{:S(2)}) %copy-start.10) | copy-done | bytes 88
  48.0 7.1 %decode.1 = (bf16[1,512,1024]{2,1,0:T(8,128)(2,1)}, bf16[16,4,1024]{2,1,0:T(4,128)(2,1)}) custom-call(s32[16,64]{1,0:T(8,128)S(1)} %copy-done.8, s32[16]{0:T(128)S(1)} %copy-done.10, bf16[16,4,1024]{2,1,0:T(4,128)(2,1)S(1)} %copy-done.3, bf16[16,4,128]{2,1,0:T(4,128)(2,1)S(1)} %copy-done.6, bf16[16,4,128]{2,1,0:T(4,128)(2,1)S(1)} %copy-done.7, ...), custom_call_target="tpu_custom_call" | custom-call | tf_op jit(solution)/shard_map/decode/pallas_call | solution.py:407
Async XLA Ops:
  0.6 1.2 %copy-start = (bf16[1,512,1024]{2,1,0:T(8,128)(2,1)S(1)}, bf16[1,512,1024]{2,1,0:T(8,128)(2,1)}, u32[]{:S(2)}) copy-start(bf16[1,512,1024]{2,1,0:T(8,128)(2,1)} %q_ref.3) | copy-start | bytes 3145732
  1.9 0.9 %copy-start.4 = (bf16[1,512,128]{2,1,0:T(8,128)(2,1)S(1)}, bf16[1,512,128]{2,1,0:T(8,128)(2,1)}, u32[]{:S(2)}) copy-start(bf16[1,512,128]{2,1,0:T(8,128)(2,1)} %param.12) | copy-start | bytes 393220
  2.8 0.9 %copy-start.5 = (bf16[1,512,128]{2,1,0:T(8,128)(2,1)S(1)}, bf16[1,512,128]{2,1,0:T(8,128)(2,1)}, u32[]{:S(2)}) copy-start(bf16[1,512,128]{2,1,0:T(8,128)(2,1)} %param.13) | copy-start | bytes 393220
  3.7 0.7 %copy-start.9 = (s32[1,16]{1,0:T(1,128)S(1)}, s32[1,16]{1,0:T(1,128)}, u32[]{:S(2)}) copy-start(s32[1,16]{1,0:T(1,128)} %owner_ref.1) | copy-start | bytes 196
  41.1 1.6 %copy-start.1 = (bf16[256,32,128]{2,1,0:T(8,128)(2,1)S(1)}, bf16[256,32,128]{2,1,0:T(8,128)(2,1)}, u32[]{:S(2)}) copy-start(bf16[256,32,128]{2,1,0:T(8,128)(2,1)} %poolk_ref.1) | copy-start | bytes 6291460
  42.7 1.6 %copy-start.2 = (bf16[256,32,128]{2,1,0:T(8,128)(2,1)S(1)}, bf16[256,32,128]{2,1,0:T(8,128)(2,1)}, u32[]{:S(2)}) copy-start(bf16[256,32,128]{2,1,0:T(8,128)(2,1)} %poolv_ref.1) | copy-start | bytes 6291460
  44.3 0.9 %copy-start.3 = (bf16[16,4,1024]{2,1,0:T(4,128)(2,1)S(1)}, bf16[16,4,1024]{2,1,0:T(4,128)(2,1)}, u32[]{:S(2)}) copy-start(bf16[16,4,1024]{2,1,0:T(4,128)(2,1)} %sq_ref.1) | copy-start | bytes 393220
  45.2 0.7 %copy-start.6 = (bf16[16,4,128]{2,1,0:T(4,128)(2,1)S(1)}, bf16[16,4,128]{2,1,0:T(4,128)(2,1)}, u32[]{:S(2)}) copy-start(bf16[16,4,128]{2,1,0:T(4,128)(2,1)} %sk_ref.1) | copy-start | bytes 49156
  45.9 0.7 %copy-start.7 = (bf16[16,4,128]{2,1,0:T(4,128)(2,1)S(1)}, bf16[16,4,128]{2,1,0:T(4,128)(2,1)}, u32[]{:S(2)}) copy-start(bf16[16,4,128]{2,1,0:T(4,128)(2,1)} %sv_ref.1) | copy-start | bytes 49156
  46.6 0.7 %copy-start.8 = (s32[16,64]{1,0:T(8,128)S(1)}, s32[16,64]{1,0:T(8,128)}, u32[]{:S(2)}) copy-start(s32[16,64]{1,0:T(8,128)} %table_ref.1) | copy-start | bytes 12292
  47.3 0.7 %copy-start.10 = (s32[16]{0:T(128)S(1)}, s32[16]{0:T(128)}, u32[]{:S(2)}) copy-start(s32[16]{0:T(128)} %length_ref.1) | copy-start | bytes 196

commit v2 on v1

v2 whole, which is shorter than its diff:
```python
import functools
import math

import jax
import jax.numpy as jnp
from jax import lax
from jax.experimental import pallas as pl
from jax.experimental.pallas import tpu as pltpu
from jax.sharding import PartitionSpec as P

MESH = pl.DeviceIdType.MESH
HD = 128
PAGE = 32
MAXPG = 64
STEPS = 4
GROUP = 8
TOK = 512
VROWS = 144
POOL = 256
REQS = 16
CTX = MAXPG * PAGE
ROWS = STEPS * GROUP
SCALE = math.log2(math.e) / math.sqrt(HD)
LIMIT = 2.0**100
LOW = -1e30
NT = (((1,), (1,)), ((), ()))


def dot_nt(a, b):
    return lax.dot_general(a, b, NT, preferred_element_type=jnp.float32)


def dot_nn(a, b):
    return jnp.dot(a, b, preferred_element_type=jnp.float32)


def prefill_kernel(
    chips, sections,
    q_hbm, k_hbm, v_hbm, owner_hbm, poolk_hbm, poolv_hbm,
    out_ref, total_ref, kall, vall, pages,
    q_ref, k_ref, v_ref, owner_ref, acc, shift, outgoing,
    ksend, vsend, krecv, vrecv, fksend, fvsend, psend, precv, asem,
):
    section = lax.axis_index("section")
    seq = lax.axis_index("seq")
    tensor = lax.axis_index("tensor")
    width = 2 * chips
    count = sections * width
    chip, core = seq // 2, seq % 2
    mate = chip * 2 + (1 - core)
    block = section * width + seq

    load_k = pltpu.make_async_copy(k_hbm, k_ref, asem.at[0])
    load_v = pltpu.make_async_copy(v_hbm, v_ref, asem.at[1])
    load_owner = pltpu.make_async_copy(owner_hbm, owner_ref, asem.at[2])
    load_q = pltpu.make_async_copy(q_hbm, q_ref, asem.at[3])
    for copy in (load_k, load_v, load_owner, load_q):
        copy.start()

    barrier = pltpu.get_barrier_semaphore()

    @pl.loop(1, count)
    def _(step):
        other = lax.rem(block + step, count)
        pl.semaphore_signal(
            barrier, inc=1,
            device_id=(other // width, lax.rem(other, width), tensor), device_id_type=MESH,
        )

    load_pool = [
        pltpu.make_async_copy(poolk_hbm, pages.at[pl.ds(0, POOL), pl.ds(0, PAGE)], asem.at[4]),
        pltpu.make_async_copy(poolv_hbm, pages.at[pl.ds(0, POOL), pl.ds(PAGE, PAGE)], asem.at[5]),
    ]
    for index in range(width):
        vall[index, HD:, :] = jnp.ones((VROWS - HD, TOK), jnp.bfloat16)
    load_v.wait()
    vall[seq, :HD, :] = v_ref[...].reshape(TOK, HD).T
    load_k.wait()
    kall[seq] = k_ref[...]
    load_owner.wait()

    def page_copy(step):
        other = lax.rem(block + step, count)
        return pltpu.make_async_remote_copy(
            src_ref=outgoing.at[other], dst_ref=pages.at[POOL + block],
            send_sem=psend.at[other], recv_sem=precv.at[block],
            device_id=(other // width, lax.rem(other, width), tensor), device_id_type=MESH,
        )

    def fill_page(target):
        place = jnp.int32(0)
        for page in range(TOK // PAGE):
            place = jnp.where(owner_ref[0, page] == target, page, place)
        outgoing[target, :PAGE, :] = k_ref[place]
        outgoing[target, PAGE:, :] = v_ref[place]

    @pl.loop(0, count)
    def _(target):
        fill_page(target)

    pl.semaphore_wait(barrier, count - 1)

    def k_copy(held, target, ssem):
        return pltpu.make_async_remote_copy(
            src_ref=kall.at[held], dst_ref=kall.at[held], send_sem=ssem, recv_sem=krecv.at[held],
            device_id=(section, target, tensor), device_id_type=MESH,
        )

    def v_copy(held, target, ssem):
        return pltpu.make_async_remote_copy(
            src_ref=vall.at[held, pl.ds(0, HD)], dst_ref=vall.at[held, pl.ds(0, HD)],
            send_sem=ssem, recv_sem=vrecv.at[held],
            device_id=(section, target, tensor), device_id_type=MESH,
        )

    def start_block(held, target, slot):
        k_copy(held, target, ksend.at[slot]).start()
        v_copy(held, target, vsend.at[slot]).start()

    def sent_block(slot):
        k_copy(seq, mate, ksend.at[slot]).wait_send()
        v_copy(seq, mate, vsend.at[slot]).wait_send()

    def got_block(held):
        k_copy(held, mate, ksend.at[0]).wait_recv()
        v_copy(held, mate, vsend.at[0]).wait_recv()

    def pass_block(held, slot):
        k_copy(held, mate, fksend.at[slot]).start()
        v_copy(held, mate, fvsend.at[slot]).start()

    def passed_block(slot):
        k_copy(seq, mate, fksend.at[slot]).wait_send()
        v_copy(seq, mate, fvsend.at[slot]).wait_send()

    up = chip < chips - 1
    down = (chip == 0) | ((chip == 1) & (core == 1))

    @pl.when(core == 0)
    def _():
        pass_block(seq, chip)

    @pl.when(up)
    def _():
        start_block(seq, (chip + 1) * 2 + core, 0)

    @pl.when(down)
    def _():
        start_block(seq, lax.rem(chip + chips - 1, chips) * 2 + core, 1)

    for copy in load_pool:
        copy.start()
    load_q.wait()

    ones = jnp.ones((8, HD), jnp.bfloat16)
    half = TOK // 2
    own_k = k_ref[...].reshape(TOK, HD)
    k_low, k_high = own_k[:half], own_k[half:]
    key_at = lax.broadcasted_iota(jnp.int32, (half, TOK), 0)
    query_at = lax.broadcasted_iota(jnp.int32, (half, TOK), 1)
    low_valid = key_at <= query_at
    high_valid = low_valid[:, :half]

    def query(head):
        return q_ref[0, :, head * HD:(head + 1) * HD]

    shifts = []
    for head in range(GROUP):
        product = (query(head).astype(jnp.float32) * own_k.astype(jnp.float32)).astype(jnp.bfloat16)
        shifts.append(dot_nt(ones, product)[:1])
    for head in range(GROUP):
        shift[head] = shifts[head]

    def own_scores(head):
        q = query(head)
        return dot_nt(k_low, q), dot_nt(k_high, q[half:])

    scores = own_scores(0)
    for head in range(GROUP):
        following = own_scores(head + 1) if head + 1 < GROUP else None
        base = shift[head]
        low = jnp.where(low_valid, jnp.exp2((scores[0] - base) * SCALE), 0.0)
        high = jnp.where(high_valid, jnp.exp2((scores[1] - base[:, half:]) * SCALE), 0.0)
        first = dot_nn(vall[seq, :, :half], low.astype(jnp.bfloat16))
        second = dot_nn(vall[seq, :, half:], high.astype(jnp.bfloat16))
        acc[head, :, :half] = first[:, :half]
        acc[head, :, half:] = first[:, half:] + second
        scores = following

    def attend(held):
        keys = kall[held].reshape(TOK, HD)
        values = vall[held]
        scores = dot_nt(keys, query(0))
        for head in range(GROUP):
            following = dot_nt(keys, query(head + 1)) if head + 1 < GROUP else None
            weights = jnp.exp2((scores - shift[head]) * SCALE).astype(jnp.bfloat16)
            acc[head] += dot_nn(values, weights)
            scores = following

    def start_pages():
        @pl.when(up)
        def _():
            sent_block(0)

        @pl.when(down)
        def _():
            sent_block(1)

        @pl.loop(1, count)
        def _(step):
            page_copy(step).start()

    relays = ((chip == 0) & (core == 1)) | ((chip == 1) & (core == 0))
    relays = relays | ((chip == 2) & (core == 0)) | ((chip == 3) & (core == 1))

    def near_blocks():
        first = (chip - 1) * 2 + core
        got_block(first)

        @pl.when((core == 0) & (chip < 3))
        def _():
            start_block(first, (chip + 1) * 2 + core, 2)

        pass_block(first, chip - 1)

        @pl.when(chip == 3)
        def _():
            got_block(core)

            @pl.when(core == 1)
            def _():
                start_block(core, 2 * 2 + core, 2)

            pass_block(core, 0)

        start_pages()

    @pl.loop(0, core + 2 * chip)
    def _(step):
        turn = step - core

        @pl.when(turn == 0)
        def _():
            near_blocks()

        last = (chip == 3) & (turn >= 4)
        edge = (chip == 3) & (turn < 4)
        far = jnp.where(edge, 2 - 2 * (turn % 2), jnp.where(last, 1, chip - 1 - turn // 2))
        straight = jnp.where(edge, turn < 2, turn % 2 == 0)
        held = jnp.where(turn < 0, mate, far * 2 + jnp.where(straight, core, 1 - core))
        beyond = (turn >= 0) & straight & ((last) | ((chip == 2) & (turn >= 2)))

        @pl.when(jnp.logical_not((turn >= 0) & straight) | beyond)
        def _():
            got_block(held)

        @pl.when(beyond)
        def _():
            pass_block(held, far)

        attend(held)

    @pl.when(chip == 0)
    def _():
        start_pages()

        @pl.when(core == 1)
        def _():
            got_block(2 + core)
            start_block(2 + core, 3 * 2 + core, 2)

    for head in range(GROUP):
        state = acc[head]
        total = state[HD:HD + 1]
        total_ref[head:head + 1, :] = total
        out_ref[0, :, head * HD:(head + 1) * HD] = (state[:HD] / total).astype(jnp.bfloat16).T

    @pl.loop(0, chip)
    def _(far):
        passed_block(far)

    @pl.when(core == 0)
    def _():
        passed_block(chip)

    @pl.when(relays)
    def _():
        sent_block(2)

    for copy in load_pool:
        copy.wait()
    pages[POOL + block] = outgoing[block]

    @pl.loop(1, count)
    def _(step):
        other = lax.rem(block + step, count)
        page_copy(step).wait_send()
        pltpu.make_async_remote_copy(
            src_ref=outgoing.at[other], dst_ref=pages.at[POOL + other],
            send_sem=psend.at[other], recv_sem=precv.at[other],
            device_id=(section, mate, tensor), device_id_type=MESH,
        ).wait_recv()


def decode_kernel(
    gang,
    table_hbm, length_hbm, sq_hbm, sk_hbm, sv_hbm, pages, early_ref, total_ref,
    q_ref, karch_ref, varch_ref,
    final_ref, out_ref,
    table_ref, length_ref, sq_ref, sk_ref, sv_ref, q_all, new_part, sems,
    q_slow, k_slow, v_slow, o_slow,
):
    sources = (early_ref, table_hbm, length_hbm, sq_hbm, sk_hbm, sv_hbm)
    targets = (final_ref, table_ref, length_ref, sq_ref, sk_ref, sv_ref)
    loads = [pltpu.make_async_copy(x, y, sems.at[i]) for i, (x, y) in enumerate(zip(sources, targets))]
    for copy in loads[1:]:
        copy.start()
    loads[0].start()
    for copy in loads[1:]:
        copy.wait()

    for r in range(REQS):
        wide = sq_ref[r].astype(jnp.float32)
        q_all[r] = jnp.concatenate(
            [wide[:, h * HD:(h + 1) * HD] for h in range(GROUP)], axis=0
        ).astype(jnp.bfloat16)
    new_k = jnp.concatenate([sk_ref[r].astype(jnp.float32) for r in range(REQS)], 0).astype(jnp.bfloat16)
    new_v = jnp.concatenate([sv_ref[r].astype(jnp.float32) for r in range(REQS)], 0).astype(jnp.bfloat16)
    new_scores = dot_nt(q_all[...].reshape(REQS * ROWS, HD), new_k)
    shape = (REQS * ROWS, REQS * STEPS)
    row = lax.broadcasted_iota(jnp.int32, shape, 0)
    column = lax.broadcasted_iota(jnp.int32, shape, 1)
    fits = (column // STEPS == row // ROWS) & (column % STEPS <= row % STEPS)
    new_part[...] = jnp.where(fits, new_scores, LOW).reshape(REQS, ROWS, REQS * STEPS)

    position = lax.broadcasted_iota(jnp.int32, (ROWS, CTX), 1)
    cut = 8

    @pl.loop(0, REQS // gang)
    def _(turn):
        scores, extras = [], []
        for g in range(gang):
            r = turn * gang + g
            q = q_all[r]
            parts = []
            for b in range(MAXPG // cut):
                keys = jnp.concatenate([pages[table_ref[r, b * cut + i], :PAGE] for i in range(cut)], axis=0)
                parts.append(dot_nt(q, keys))
            scores.append(jnp.where(position < length_ref[r], jnp.concatenate(parts, axis=1), LOW))
            extras.append(new_part[r])
        for g in range(gang):
            r = turn * gang + g
            top = jnp.maximum(
                jnp.max(scores[g], axis=1, keepdims=True), jnp.max(extras[g], axis=1, keepdims=True)
            )
            weights = jnp.exp2((scores[g] - top) * SCALE)
            extra = jnp.exp2((extras[g] - top) * SCALE)
            total = jnp.sum(weights, axis=1, keepdims=True) + jnp.sum(extra, axis=1, keepdims=True)
            weights = weights.astype(jnp.bfloat16)
            summed = dot_nn(extra.astype(jnp.bfloat16), new_v)
            for b in range(MAXPG // cut):
                values = jnp.concatenate([pages[table_ref[r, b * cut + i], PAGE:] for i in range(cut)], axis=0)
                summed += dot_nn(weights[:, b * cut * PAGE:(b + 1) * cut * PAGE], values)
            result = summed / total
            out_ref[r] = jnp.concatenate(
                [result[h * STEPS:(h + 1) * STEPS] for h in range(GROUP)], axis=1
            ).astype(jnp.bfloat16)

    loads[0].wait()

    fine = jnp.min(jnp.where(total_ref[...] < LIMIT, 1.0, 0.0)) > 0.5

    @pl.when(jnp.logical_not(fine))
    def _():
        seq = lax.axis_index("seq")
        load = pltpu.make_async_copy(q_ref, q_slow, sems.at[0])
        load.start()
        load.wait()
        key_at = lax.broadcasted_iota(jnp.int32, (TOK, TOK), 0)
        query_at = lax.broadcasted_iota(jnp.int32, (TOK, TOK), 1)
        for head in range(GROUP):
            q = q_slow[0, :, head * HD:(head + 1) * HD]

            def advance(held, state):
                top, state_acc = state
                loads = (
                    pltpu.make_async_copy(karch_ref.at[held], k_slow, sems.at[1]),
                    pltpu.make_async_copy(varch_ref.at[held], v_slow, sems.at[2]),
                )
                for copy in loads:
                    copy.start()
                for copy in loads:
                    copy.wait()
                valid = key_at + held * TOK <= query_at + seq * TOK
                s = jnp.where(valid, dot_nt(k_slow[...].reshape(TOK, HD), q), LOW)
                fresh = jnp.maximum(top, jnp.max(s, axis=0, keepdims=True))
                w = jnp.exp2((s - fresh) * SCALE).astype(jnp.bfloat16)
                return fresh, state_acc * jnp.exp2((top - fresh) * SCALE) + dot_nn(v_slow[...], w)

            start = (jnp.full((1, TOK), LOW, jnp.float32), jnp.zeros((VROWS, TOK), jnp.float32))
            _, state = lax.fori_loop(0, seq + 1, lambda i, s: advance(seq - i, s), start)
            o_slow[0, :, head * HD:(head + 1) * HD] = (state[:HD] / state[HD:HD + 1]).astype(jnp.bfloat16).T
        store = pltpu.make_async_copy(o_slow, final_ref, sems.at[0])
        store.start()
        store.wait()


def in_hbm(array):
    return pltpu.with_memory_space_constraint(array, pltpu.HBM)


def on_device(
    prompt_query, prompt_keys, prompt_values, page_owner, pool_keys, pool_values,
    step_query, step_keys, step_values, page_table, context_len,
):
    sections = lax.axis_size("section")
    width = lax.axis_size("seq")
    count = sections * width
    chips = width // 2
    bf16, f32 = jnp.bfloat16, jnp.float32
    vmem = pl.BlockSpec(memory_space=pltpu.VMEM)
    hbm = pl.BlockSpec(memory_space=pltpu.HBM)
    anywhere = pl.BlockSpec(memory_space=pl.ANY)
    pages = TOK // PAGE
    dma = pltpu.SemaphoreType.DMA
    early, totals, karch, varch, held_pages = pl.pallas_call(
        functools.partial(prefill_kernel, chips, sections),
        out_shape=(
            jax.ShapeDtypeStruct((1, TOK, GROUP * HD), bf16),
            jax.ShapeDtypeStruct((GROUP, TOK), f32),
            jax.ShapeDtypeStruct((width, pages, PAGE, HD), bf16),
            jax.ShapeDtypeStruct((width, VROWS, TOK), bf16),
            jax.ShapeDtypeStruct((POOL + count, 2 * PAGE, HD), bf16),
        ),
        in_specs=[hbm] * 6,
        out_specs=(vmem,) * 5,
        scratch_shapes=[
            pltpu.VMEM((1, TOK, GROUP * HD), bf16),
            pltpu.VMEM((pages, PAGE, HD), bf16),
            pltpu.VMEM((pages, PAGE, HD), bf16),
            pltpu.SMEM((1, pages), jnp.int32),
            pltpu.VMEM((GROUP, VROWS, TOK), f32),
            pltpu.VMEM((GROUP, 1, TOK), f32),
            pltpu.VMEM((count, 2 * PAGE, HD), bf16),
            dma((3,)), dma((3,)), dma((width,)), dma((width,)),
            dma((chips,)), dma((chips,)), dma((count,)), dma((count,)),
            dma((6,)),
        ],
        compiler_params=pltpu.CompilerParams(
            collective_id=0, has_side_effects=True, vmem_limit_bytes=32 * 2**20
        ),
        name="prefill",
    )(
        in_hbm(prompt_query),
        in_hbm(prompt_keys.reshape(pages, PAGE, HD)),
        in_hbm(prompt_values.reshape(pages, PAGE, HD)),
        in_hbm(page_owner),
        in_hbm(pool_keys),
        in_hbm(pool_values),
    )
    return pl.pallas_call(
        functools.partial(decode_kernel, 4),
        out_shape=(
            jax.ShapeDtypeStruct((1, TOK, GROUP * HD), bf16),
            jax.ShapeDtypeStruct((REQS, STEPS, GROUP * HD), bf16),
        ),
        in_specs=[hbm] * 5 + [vmem, anywhere, vmem, hbm, anywhere, anywhere],
        out_specs=(hbm, vmem),
        scratch_shapes=[
            pltpu.SMEM((REQS, MAXPG), jnp.int32),
            pltpu.SMEM((REQS,), jnp.int32),
            pltpu.VMEM((REQS, STEPS, GROUP * HD), bf16),
            pltpu.VMEM((REQS, STEPS, HD), bf16),
            pltpu.VMEM((REQS, STEPS, HD), bf16),
            pltpu.VMEM((REQS, ROWS, HD), bf16),
            pltpu.VMEM((REQS, ROWS, REQS * STEPS), f32),
            dma((6,)),
            pltpu.VMEM((1, TOK, GROUP * HD), bf16),
            pltpu.VMEM((pages, PAGE, HD), bf16),
            pltpu.VMEM((VROWS, TOK), bf16),
            pltpu.VMEM((1, TOK, GROUP * HD), bf16),
        ],
        compiler_params=pltpu.CompilerParams(vmem_limit_bytes=32 * 2**20),
        name="decode",
    )(
        in_hbm(page_table), in_hbm(context_len), in_hbm(step_query), in_hbm(step_keys), in_hbm(step_values),
        held_pages, early, totals, in_hbm(prompt_query), karch, varch,
    )


def solution(mesh):
    in_specs = (
        P("section", "seq", "tensor"),
        P("section", "seq", "tensor"),
        P("section", "seq", "tensor"),
        P("section", "seq"),
        P(("section", "seq"), None, "tensor"),
        P(("section", "seq"), None, "tensor"),
        P(("section", "seq"), None, "tensor"),
        P(("section", "seq"), None, "tensor"),
        P(("section", "seq"), None, "tensor"),
        P(("section", "seq"), None),
        P(("section", "seq")),
    )
    out_specs = (P("section", "seq", "tensor"), P(("section", "seq"), None, "tensor"))
    return jax.shard_map(
        on_device, mesh=mesh, in_specs=in_specs, out_specs=out_specs, check_vma=False
    )
```

time: 55.7 us -> 36 us (0.65)
  the two profiles are of different devices: /device:TPU:120 before, /device:TPU:113 now
where the time goes in v2:
time: 36 us; the launch traced here: 35.8 us
  Pallas kernels  35.2 us (98%)
  between operations  0.64 us (2%)
    pallas_call x1, Pallas kernels, on_device(): pl.pallas_call(functools.partial(prefill_kernel, chips, sections), out_sh...  28.4 us
    pallas_call x1, Pallas kernels, on_device(): pl.pallas_call(functools.partial(decode_kernel, 4), out_shape=(jax.ShapeD...  6.76 us

profile of v2, /device:TPU:113, one launch (start us, length us, event | category | flops | bytes accessed | tf_op | source)
XLA Modules:
  0.0 35.8 jit_solution(16964772023954362974)
XLA Ops:
  0.6 28.4 %prefill.1 = (bf16[1,512,1024]{2,1,0:T(8,128)(2,1)S(1)}, f32[8,512]{1,0:T(8,128)S(1)}, bf16[8,16,32,128]{3,2,1,0:T(8,128)(2,1)S(1)}, bf16[8,144,512]{2,1,0:T(8,128)(2,1)S(1)}, bf16[288,64,128]{2,1,0:T(8,128)(2,1)S(1)}) custom-call(bf16[1,512,1024]{2,1,0:T(8,128)(2,1)} %q_ref.1, bf16[16,32,128]{2,1,0:T(8,128)(2,1)} %bitcast.2, bf16[16,32,128]{2,1,0:T(8,128)(2,1)} %bitcast.3, ...), custom_call_target="tpu_custom_call" | custom-call | tf_op jit(solution)/shard_map/prefill/pallas_call | solution.py:426
  29.1 6.8 %decode.1 = (bf16[1,512,1024]{2,1,0:T(8,128)(2,1)}, bf16[16,4,1024]{2,1,0:T(4,128)(2,1)}) custom-call(s32[16,64]{1,0:T(8,128)} %table_hbm.1, s32[16]{0:T(128)} %length_hbm.1, bf16[16,4,1024]{2,1,0:T(4,128)(2,1)} %sq_hbm.1, bf16[16,4,128]{2,1,0:T(4,128)(2,1)} %sk_hbm.1, bf16[16,4,128]{2,1,0:T(4,128)(2,1)} %sv_hbm.1, ...), custom_call_target="tpu_custom_call" | custom-call | tf_op jit(solution)/shard_map/decode/pallas_call | solution.py:461

commit v3 on v2

v3 whole, which is shorter than its diff:
```python
import functools
import math

import jax
import jax.numpy as jnp
from jax import lax
from jax.experimental import pallas as pl
from jax.experimental.pallas import tpu as pltpu
from jax.sharding import PartitionSpec as P

MESH = pl.DeviceIdType.MESH
HD = 128
PAGE = 32
MAXPG = 64
STEPS = 4
GROUP = 8
TOK = 512
VROWS = 144
HALF = TOK // 2
SLABS = HALF // PAGE
POOL = 256
REQS = 16
CTX = MAXPG * PAGE
ROWS = STEPS * GROUP
SCALE = math.log2(math.e) / math.sqrt(HD)
LIMIT = 2.0**100
LOW = -1e30
NT = (((1,), (1,)), ((), ()))


def dot_nt(a, b):
    return lax.dot_general(a, b, NT, preferred_element_type=jnp.float32)


def dot_nn(a, b):
    return jnp.dot(a, b, preferred_element_type=jnp.float32)


def prefill_kernel(
    chips, sections,
    q_hbm, k_hbm, v_hbm, owner_hbm, poolk_hbm, poolv_hbm, sq_hbm, sk_hbm, sv_hbm,
    out_ref, total_ref, kall, vall, pages, q_all, new_part, new_v,
    sq_ref, sk_ref, sv_ref, q_ref, own, prev, following, beyond, passed,
    table0, table1, table2, table3, owner0, owner1, owner2, owner3,
    acc, shift, outgoing,
    nsend, rsend, drecv, msend, mrecv, tsend, trecv, psend, precv, asem,
):
    section = lax.axis_index("section")
    seq = lax.axis_index("seq")
    tensor = lax.axis_index("tensor")
    width = 2 * chips
    chip, core = seq // 2, seq % 2
    mate = chip * 2 + (1 - core)
    block = section * width + seq
    above = lax.rem(chip + 1, chips)
    below = lax.rem(chip + chips - 1, chips)
    across = lax.rem(chip + 2, chips)
    origin = (chip, below, above, across)
    held = tuple(c * 2 + core for c in origin)
    direct = (own, prev, following, beyond)
    tables = (table0, table1, table2, table3)
    owners = (owner0, owner1, owner2, owner3)

    def place(row, target):
        return (row, target, tensor)

    loads = [
        pltpu.make_async_copy(k_hbm, own.at[0], asem.at[0]),
        pltpu.make_async_copy(v_hbm, own.at[1], asem.at[1]),
        pltpu.make_async_copy(owner_hbm, table0, asem.at[2]),
        pltpu.make_async_copy(owner_hbm, owner0, asem.at[3]),
        pltpu.make_async_copy(sq_hbm, sq_ref, asem.at[10]),
        pltpu.make_async_copy(sk_hbm, sk_ref, asem.at[11]),
        pltpu.make_async_copy(sv_hbm, sv_ref, asem.at[12]),
        pltpu.make_async_copy(q_hbm, q_ref, asem.at[4]),
    ]
    load_pool = [
        pltpu.make_async_copy(poolk_hbm, pages.at[pl.ds(0, POOL), pl.ds(0, PAGE)], asem.at[5]),
        pltpu.make_async_copy(poolv_hbm, pages.at[pl.ds(0, POOL), pl.ds(PAGE, PAGE)], asem.at[6]),
    ]
    for copy in loads:
        copy.start()

    barrier = pltpu.get_barrier_semaphore()
    peers = [place(section, above * 2 + core), place(section, below * 2 + core), place(section, mate)]
    for offset in range(1, sections):
        for other in range(2):
            peers.append(place(lax.rem(section + offset, sections), chip * 2 + other))
    for peer in peers:
        pl.semaphore_signal(barrier, inc=1, device_id=peer, device_id_type=MESH)

    for index in range(2 * width):
        vall[index, HD:, :] = jnp.ones((VROWS - HD, HALF), jnp.bfloat16)
    for copy in loads[:7]:
        copy.wait()
    prepare(sq_ref, sk_ref, sv_ref, q_all, new_part, new_v)
    pl.semaphore_wait(barrier, len(peers))

    def part(ref, half):
        return ref.at[:, pl.ds(half * SLABS, SLABS)]

    def near_copy(up, half):
        return pltpu.make_async_remote_copy(
            src_ref=part(own, half), dst_ref=part(prev if up else following, half),
            send_sem=nsend.at[0 if up else 1, half], recv_sem=drecv.at[1 if up else 2, half],
            device_id=place(section, (above if up else below) * 2 + core), device_id_type=MESH,
        )

    def near_table(up):
        return pltpu.make_async_remote_copy(
            src_ref=table0, dst_ref=table1 if up else table2,
            send_sem=tsend.at[0 if up else 1], recv_sem=trecv.at[1 if up else 2],
            device_id=place(section, (above if up else below) * 2 + core), device_id_type=MESH,
        )

    def relay_copy(up, half):
        return pltpu.make_async_remote_copy(
            src_ref=part(prev if up else following, half), dst_ref=part(beyond, half),
            send_sem=rsend.at[half], recv_sem=drecv.at[3, half],
            device_id=place(section, (above if up else below) * 2 + core), device_id_type=MESH,
        )

    def relay_table(up):
        return pltpu.make_async_remote_copy(
            src_ref=table1 if up else table2, dst_ref=table3,
            send_sem=tsend.at[2], recv_sem=trecv.at[3],
            device_id=place(section, (above if up else below) * 2 + core), device_id_type=MESH,
        )

    def mate_copy(kind, half):
        return pltpu.make_async_remote_copy(
            src_ref=part(direct[kind], half), dst_ref=part(passed.at[kind], half),
            send_sem=msend.at[kind, half], recv_sem=mrecv.at[kind, half],
            device_id=place(section, mate), device_id_type=MESH,
        )

    def page_copy(kind, offset, other):
        row = lax.rem(section + offset, sections)
        return pltpu.make_async_remote_copy(
            src_ref=outgoing.at[kind, offset * 2 + other],
            dst_ref=pages.at[POOL + section * width + held[kind]],
            send_sem=psend.at[kind, offset * 2 + other],
            recv_sem=precv.at[section * width + held[kind]],
            device_id=place(row, chip * 2 + other), device_id_type=MESH,
        )

    def local_owners(kind):
        return pltpu.make_async_copy(tables[kind], owners[kind], asem.at[6 + kind])

    def send_pages(kind):
        for offset in range(sections):
            for other in range(2):
                row = lax.rem(section + offset, sections)
                taker = row * width + chip * 2 + other
                slot = jnp.int32(0)
                for page in range(TOK // PAGE):
                    slot = jnp.where(owners[kind][0, page] == taker, page, slot)
                outgoing[kind, offset * 2 + other, :PAGE, :] = direct[kind][0, slot]
                outgoing[kind, offset * 2 + other, PAGE:, :] = direct[kind][1, slot]
        for offset in range(1, sections):
            for other in range(2):
                page_copy(kind, offset, other).start()
        for other in range(2):
            @pl.when(core == other)
            def _():
                pages[POOL + section * width + held[kind]] = outgoing[kind, other]

            @pl.when(core != other)
            def _():
                page_copy(kind, 0, other).start()

    for half in range(2):
        near_copy(True, half).start()
        near_copy(False, half).start()
    near_table(True).start()
    near_table(False).start()

    @pl.when(core == 0)
    def _():
        mate_copy(0, 0).start()
        mate_copy(0, 1).start()

    for copy in load_pool:
        copy.start()

    def slab(half):
        return slice(half * SLABS, (half + 1) * SLABS)

    for half in range(2):
        kall[seq * 2 + half] = own[0, slab(half)]
        vall[seq * 2 + half, :HD, :] = own[1, slab(half)].reshape(HALF, HD).T
    loads[7].wait()

    ones = jnp.ones((8, HD), jnp.bfloat16)
    own_k = own[0].reshape(TOK, HD)
    k_low, k_high = own_k[:HALF], own_k[HALF:]
    key_at = lax.broadcasted_iota(jnp.int32, (HALF, TOK), 0)
    query_at = lax.broadcasted_iota(jnp.int32, (HALF, TOK), 1)
    low_valid = key_at <= query_at
    high_valid = low_valid[:, :HALF]

    def query(head):
        return q_ref[0, :, head * HD:(head + 1) * HD]

    shifts = []
    for head in range(GROUP):
        product = (query(head).astype(jnp.float32) * own_k.astype(jnp.float32)).astype(jnp.bfloat16)
        shifts.append(dot_nt(ones, product)[:1])
    for head in range(GROUP):
        shift[head] = shifts[head]

    def own_scores(head):
        q = query(head)
        return dot_nt(k_low, q), dot_nt(k_high, q[HALF:])

    scores = own_scores(0)
    for head in range(GROUP):
        upcoming = own_scores(head + 1) if head + 1 < GROUP else None
        base = shift[head]
        low = jnp.where(low_valid, jnp.exp2((scores[0] - base) * SCALE), 0.0)
        high = jnp.where(high_valid, jnp.exp2((scores[1] - base[:, HALF:]) * SCALE), 0.0)
        first = dot_nn(vall[seq * 2], low.astype(jnp.bfloat16))
        second = dot_nn(vall[seq * 2 + 1], high.astype(jnp.bfloat16))
        acc[head, :, :HALF] = first[:, :HALF]
        acc[head, :, HALF:] = first[:, HALF:] + second
        scores = upcoming

    def attend(first, second):
        keys = jnp.concatenate([kall[first].reshape(HALF, HD), kall[second].reshape(HALF, HD)], axis=0)
        values = jnp.concatenate([vall[first], vall[second]], axis=1)
        scores = dot_nt(keys, query(0))
        for head in range(GROUP):
            upcoming = dot_nt(keys, query(head + 1)) if head + 1 < GROUP else None
            weights = jnp.exp2((scores - shift[head]) * SCALE).astype(jnp.bfloat16)
            acc[head] += dot_nn(values, weights)
            scores = upcoming

    def take(kind, half):
        kall[held[kind] * 2 + half] = direct[kind][0, slab(half)]
        vall[held[kind] * 2 + half, :HD, :] = direct[kind][1, slab(half)].reshape(HALF, HD).T

    def arrive(kind, half):
        pltpu.make_async_remote_copy(
            src_ref=part(own, half), dst_ref=part(direct[kind], half),
            send_sem=rsend.at[half], recv_sem=drecv.at[kind, half],
            device_id=place(section, mate), device_id_type=MESH,
        ).wait_recv()
        if kind < 3:
            @pl.when(core == kind - 1)
            def _():
                relay_copy(kind == 1, half).start()

        @pl.when(origin[kind] < chip)
        def _():
            mate_copy(kind, half).start()
            take(kind, half)

    def forward_pages(kind):
        pltpu.make_async_remote_copy(
            src_ref=table0, dst_ref=tables[kind], send_sem=tsend.at[2], recv_sem=trecv.at[kind],
            device_id=place(section, mate), device_id_type=MESH,
        ).wait_recv()
        if kind < 3:
            @pl.when(core == kind - 1)
            def _():
                relay_table(kind == 1).start()
        local_owners(kind).start()
        local_owners(kind).wait()
        send_pages(kind)

    edge = chip == chips - 1
    second_turn = jnp.where(edge, 2, 0)
    far_turn = jnp.where(chip == 0, 1, chip)

    @pl.loop(0, core + jnp.maximum(2 * chip, 2))
    def _(step):
        turn = step - core

        @pl.when(turn == 0)
        def _():
            arrive(1, 0)
            arrive(2, 0)
            send_pages(0)

        @pl.when(turn == second_turn)
        def _():
            arrive(1, 1)
            arrive(2, 1)
            forward_pages(1)
            forward_pages(2)

        @pl.when(turn == far_turn)
        def _():
            arrive(3, 0)
            arrive(3, 1)
            forward_pages(3)

        both = edge & (turn >= 0) & (turn < 4)
        single = jnp.where(turn < 0, 0, jnp.where(turn < 2, 1, 3))
        single = jnp.where(edge & (turn >= 4), 3, single)
        kinds = (jnp.where(both, 1, single), jnp.where(both, 2, single))
        halves = (jnp.where(both, turn // 2, 0), jnp.where(both, turn // 2, 1))
        straight = (turn >= 0) & (turn % 2 == 0)
        wanted = (turn < 0) | (turn < 2 * chip)
        indices = []
        for kind, half in zip(kinds, halves):
            move = jnp.where(kind == 1, chips - 1, jnp.where(kind == 2, 1, jnp.where(kind == 3, 2, 0)))
            index = (lax.rem(chip + move, chips) * 2 + jnp.where(straight, core, 1 - core)) * 2 + half
            indices.append(index)

            @pl.when(wanted & jnp.logical_not(straight))
            def _():
                pltpu.make_async_remote_copy(
                    src_ref=part(own, 0), dst_ref=part(passed.at[kind], half),
                    send_sem=rsend.at[0], recv_sem=mrecv.at[kind, half],
                    device_id=place(section, mate), device_id_type=MESH,
                ).wait_recv()
                kall[index] = passed[kind, 0, pl.ds(half * SLABS, SLABS)]
                vall[index, :HD, :] = passed[kind, 1, pl.ds(half * SLABS, SLABS)].reshape(HALF, HD).T

        @pl.when(wanted)
        def _():
            attend(*indices)

    for head in range(GROUP):
        state = acc[head]
        total = state[HD:HD + 1]
        total_ref[head:head + 1, :] = total
        out_ref[0, :, head * HD:(head + 1) * HD] = (state[:HD] * (1.0 / total)).astype(jnp.bfloat16).T

    for up in (True, False):
        near_table(up).wait_send()
        for half in range(2):
            near_copy(up, half).wait_send()
    relay_table(True).wait_send()
    for half in range(2):
        relay_copy(True, half).wait_send()

        @pl.when(core == 0)
        def _():
            mate_copy(0, half).wait_send()

        for kind in (1, 2, 3):
            @pl.when(origin[kind] < chip)
            def _():
                mate_copy(kind, half).wait_send()

    for copy in load_pool:
        copy.wait()

    for kind in range(4):
        for offset in range(1, sections):
            for other in range(2):
                page_copy(kind, offset, other).wait_send()
        for other in range(2):
            @pl.when(core != other)
            def _():
                page_copy(kind, 0, other).wait_send()

    @pl.loop(0, sections)
    def _(row):
        @pl.loop(0, width)
        def _(far):
            @pl.when((row != section) | (far % 2 != core))
            def _():
                pltpu.make_async_remote_copy(
                    src_ref=outgoing.at[0, 0], dst_ref=pages.at[POOL + row * width + far],
                    send_sem=psend.at[0, 0], recv_sem=precv.at[row * width + far],
                    device_id=place(section, mate), device_id_type=MESH,
                ).wait_recv()


def prepare(sq_ref, sk_ref, sv_ref, q_all, new_part, new_v):
    for r in range(REQS):
        wide = sq_ref[r].astype(jnp.float32)
        q_all[r] = jnp.concatenate(
            [wide[:, h * HD:(h + 1) * HD] for h in range(GROUP)], axis=0
        ).astype(jnp.bfloat16)
    new_k = jnp.concatenate([sk_ref[r].astype(jnp.float32) for r in range(REQS)], 0).astype(jnp.bfloat16)
    new_v[...] = jnp.concatenate([sv_ref[r].astype(jnp.float32) for r in range(REQS)], 0).astype(jnp.bfloat16)
    new_scores = dot_nt(q_all[...].reshape(REQS * ROWS, HD), new_k)
    shape = (REQS * ROWS, REQS * STEPS)
    row = lax.broadcasted_iota(jnp.int32, shape, 0)
    column = lax.broadcasted_iota(jnp.int32, shape, 1)
    fits = (column // STEPS == row // ROWS) & (column % STEPS <= row % STEPS)
    new_part[...] = jnp.where(fits, new_scores, LOW).reshape(REQS, ROWS, REQS * STEPS)


def decode_kernel(
    gang,
    table_hbm, length_hbm, pages, q_all, new_part, new_v, early_ref, total_ref,
    q_ref, karch_ref, varch_ref,
    final_ref, out_ref,
    table_ref, length_ref, sems, q_slow, k_slow, v_slow, o_slow,
):
    loads = [
        pltpu.make_async_copy(early_ref, final_ref, sems.at[0]),
        pltpu.make_async_copy(table_hbm, table_ref, sems.at[1]),
        pltpu.make_async_copy(length_hbm, length_ref, sems.at[2]),
    ]
    for copy in loads[1:]:
        copy.start()
    loads[0].start()
    for copy in loads[1:]:
        copy.wait()

    position = lax.broadcasted_iota(jnp.int32, (ROWS, CTX), 1)
    cut = 8

    @pl.loop(0, REQS // gang)
    def _(turn):
        scores, extras = [], []
        for g in range(gang):
            r = turn * gang + g
            q = q_all[r]
            parts = []
            for b in range(MAXPG // cut):
                keys = jnp.concatenate([pages[table_ref[r, b * cut + i], :PAGE] for i in range(cut)], axis=0)
                parts.append(dot_nt(q, keys))
            scores.append(jnp.where(position < length_ref[r], jnp.concatenate(parts, axis=1), LOW))
            extras.append(new_part[r])
        for g in range(gang):
            r = turn * gang + g
            top = jnp.maximum(
                jnp.max(scores[g], axis=1, keepdims=True), jnp.max(extras[g], axis=1, keepdims=True)
            )
            weights = jnp.exp2((scores[g] - top) * SCALE)
            extra = jnp.exp2((extras[g] - top) * SCALE)
            total = jnp.sum(weights, axis=1, keepdims=True) + jnp.sum(extra, axis=1, keepdims=True)
            weights = weights.astype(jnp.bfloat16)
            summed = dot_nn(extra.astype(jnp.bfloat16), new_v[...])
            for b in range(MAXPG // cut):
                values = jnp.concatenate([pages[table_ref[r, b * cut + i], PAGE:] for i in range(cut)], axis=0)
                summed += dot_nn(weights[:, b * cut * PAGE:(b + 1) * cut * PAGE], values)
            result = summed / total
            out_ref[r] = jnp.concatenate(
                [result[h * STEPS:(h + 1) * STEPS] for h in range(GROUP)], axis=1
            ).astype(jnp.bfloat16)

    loads[0].wait()

    fine = jnp.min(jnp.where(total_ref[...] < LIMIT, 1.0, 0.0)) > 0.5

    @pl.when(jnp.logical_not(fine))
    def _():
        seq = lax.axis_index("seq")
        load = pltpu.make_async_copy(q_ref, q_slow, sems.at[0])
        load.start()
        load.wait()
        key_at = lax.broadcasted_iota(jnp.int32, (HALF, TOK), 0)
        query_at = lax.broadcasted_iota(jnp.int32, (HALF, TOK), 1)
        for head in range(GROUP):
            q = q_slow[0, :, head * HD:(head + 1) * HD]

            def advance(held, state):
                top, state_acc = state
                loads = (
                    pltpu.make_async_copy(karch_ref.at[held], k_slow, sems.at[1]),
                    pltpu.make_async_copy(varch_ref.at[held], v_slow, sems.at[2]),
                )
                for copy in loads:
                    copy.start()
                for copy in loads:
                    copy.wait()
                valid = key_at + held * HALF <= query_at + seq * TOK
                s = jnp.where(valid, dot_nt(k_slow[...].reshape(HALF, HD), q), LOW)
                fresh = jnp.maximum(top, jnp.max(s, axis=0, keepdims=True))
                w = jnp.exp2((s - fresh) * SCALE).astype(jnp.bfloat16)
                return fresh, state_acc * jnp.exp2((top - fresh) * SCALE) + dot_nn(v_slow[...], w)

            start = (jnp.full((1, TOK), LOW, jnp.float32), jnp.zeros((VROWS, TOK), jnp.float32))
            _, state = lax.fori_loop(0, 2 * seq + 2, advance, start)
            o_slow[0, :, head * HD:(head + 1) * HD] = (state[:HD] / state[HD:HD + 1]).astype(jnp.bfloat16).T
        store = pltpu.make_async_copy(o_slow, final_ref, sems.at[0])
        store.start()
        store.wait()


def in_hbm(array):
    return pltpu.with_memory_space_constraint(array, pltpu.HBM)


def on_device(
    prompt_query, prompt_keys, prompt_values, page_owner, pool_keys, pool_values,
    step_query, step_keys, step_values, page_table, context_len,
):
    sections = lax.axis_size("section")
    width = lax.axis_size("seq")
    count = sections * width
    chips = width // 2
    bf16, f32 = jnp.bfloat16, jnp.float32
    vmem = pl.BlockSpec(memory_space=pltpu.VMEM)
    hbm = pl.BlockSpec(memory_space=pltpu.HBM)
    anywhere = pl.BlockSpec(memory_space=pl.ANY)
    pages = TOK // PAGE
    dma = pltpu.SemaphoreType.DMA
    early, totals, karch, varch, held_pages, q_all, new_part, new_v = pl.pallas_call(
        functools.partial(prefill_kernel, chips, sections),
        out_shape=(
            jax.ShapeDtypeStruct((1, TOK, GROUP * HD), bf16),
            jax.ShapeDtypeStruct((GROUP, TOK), f32),
            jax.ShapeDtypeStruct((2 * width, SLABS, PAGE, HD), bf16),
            jax.ShapeDtypeStruct((2 * width, VROWS, HALF), bf16),
            jax.ShapeDtypeStruct((POOL + count, 2 * PAGE, HD), bf16),
            jax.ShapeDtypeStruct((REQS, ROWS, HD), bf16),
            jax.ShapeDtypeStruct((REQS, ROWS, REQS * STEPS), f32),
            jax.ShapeDtypeStruct((REQS * STEPS, HD), bf16),
        ),
        in_specs=[hbm] * 9,
        out_specs=(vmem,) * 8,
        scratch_shapes=[
            pltpu.VMEM((REQS, STEPS, GROUP * HD), bf16),
            pltpu.VMEM((REQS, STEPS, HD), bf16),
            pltpu.VMEM((REQS, STEPS, HD), bf16),
            pltpu.VMEM((1, TOK, GROUP * HD), bf16),
            *[pltpu.VMEM((2, pages, PAGE, HD), bf16)] * 4,
            pltpu.VMEM((4, 2, pages, PAGE, HD), bf16),
            *[pltpu.VMEM((1, pages), jnp.int32)] * 4,
            *[pltpu.SMEM((1, pages), jnp.int32)] * 4,
            pltpu.VMEM((GROUP, VROWS, TOK), f32),
            pltpu.VMEM((GROUP, 1, TOK), f32),
            pltpu.VMEM((4, 2 * sections, 2 * PAGE, HD), bf16),
            dma((2, 2)), dma((2,)), dma((4, 2)), dma((4, 2)), dma((4, 2)),
            dma((3,)), dma((4,)), dma((4, 2 * sections)), dma((count,)),
            dma((13,)),
        ],
        compiler_params=pltpu.CompilerParams(
            collective_id=0, has_side_effects=True, vmem_limit_bytes=32 * 2**20
        ),
        name="prefill",
    )(
        in_hbm(prompt_query),
        in_hbm(prompt_keys.reshape(pages, PAGE, HD)),
        in_hbm(prompt_values.reshape(pages, PAGE, HD)),
        in_hbm(page_owner),
        in_hbm(pool_keys),
        in_hbm(pool_values),
        in_hbm(step_query),
        in_hbm(step_keys),
        in_hbm(step_values),
    )
    return pl.pallas_call(
        functools.partial(decode_kernel, REQS),
        out_shape=(
            jax.ShapeDtypeStruct((1, TOK, GROUP * HD), bf16),
            jax.ShapeDtypeStruct((REQS, STEPS, GROUP * HD), bf16),
        ),
        in_specs=[hbm] * 2 + [vmem] * 4 + [anywhere, vmem, hbm, anywhere, anywhere],
        out_specs=(hbm, vmem),
        scratch_shapes=[
            pltpu.SMEM((REQS, MAXPG), jnp.int32),
            pltpu.SMEM((REQS,), jnp.int32),
            dma((3,)),
            pltpu.VMEM((1, TOK, GROUP * HD), bf16),
            pltpu.VMEM((SLABS, PAGE, HD), bf16),
            pltpu.VMEM((VROWS, HALF), bf16),
            pltpu.VMEM((1, TOK, GROUP * HD), bf16),
        ],
        compiler_params=pltpu.CompilerParams(vmem_limit_bytes=32 * 2**20),
        name="decode",
    )(
        in_hbm(page_table), in_hbm(context_len), held_pages, q_all, new_part, new_v,
        early, totals, in_hbm(prompt_query), karch, varch,
    )


def solution(mesh):
    in_specs = (
        P("section", "seq", "tensor"),
        P("section", "seq", "tensor"),
        P("section", "seq", "tensor"),
        P("section", "seq"),
        P(("section", "seq"), None, "tensor"),
        P(("section", "seq"), None, "tensor"),
        P(("section", "seq"), None, "tensor"),
        P(("section", "seq"), None, "tensor"),
        P(("section", "seq"), None, "tensor"),
        P(("section", "seq"), None),
        P(("section", "seq")),
    )
    out_specs = (P("section", "seq", "tensor"), P(("section", "seq"), None, "tensor"))
    return jax.shard_map(
        on_device, mesh=mesh, in_specs=in_specs, out_specs=out_specs, check_vma=False
    )
```

time: 36 us -> 33.6 us (0.933)
  the two profiles are of different devices: /device:TPU:113 before, /device:TPU:120 now
where the time goes in v3:
time: 33.6 us; the launch traced here: 33.4 us
  Pallas kernels  32.8 us (98%)
  between operations  0.64 us (2%)
    pallas_call x1, Pallas kernels, on_device(): pl.pallas_call(functools.partial(prefill_kernel, chips, sections), out_sh...  26.5 us
    pallas_call x1, Pallas kernels, on_device(): pl.pallas_call(functools.partial(decode_kernel, REQS), out_shape=(jax.Sha...  6.26 us

profile of v3, /device:TPU:120, one launch (start us, length us, event | category | flops | bytes accessed | tf_op | source)
XLA Modules:
  0.0 33.4 jit_solution(17439433753020755405)
XLA Ops:
  0.6 26.5 %prefill.1 = (bf16[1,512,1024]{2,1,0:T(8,128)(2,1)S(1)}, f32[8,512]{1,0:T(8,128)S(1)}, bf16[16,8,32,128]{3,2,1,0:T(8,128)(2,1)S(1)}, bf16[16,144,256]{2,1,0:T(8,...) custom-call(bf16[1,512,1024]{2,1,0:T(8,128)(2,1)} %q_ref.1, ...), custom_call_target="tpu_custom_call" | custom-call | tf_op jit(solution)/shard_map/prefill/pallas_call | solution.py:497
  27.2 6.3 %decode.1 = (bf16[1,512,1024]{2,1,0:T(8,128)(2,1)}, bf16[16,4,1024]{2,1,0:T(4,128)(2,1)}) custom-call(s32[16,64]{1,0:T(8,128)} %table_hbm.1, s32[16]{0:T(128)} %length_hbm.1, bf16[288,64,128]{2,1,0:T(8,128)(2,1)S(1)} %get-tuple-element.10.pages, bf16[16,32,128]{2,1,0:T(8,128)(2,1)S(1)} %get-tuple-element.11.q_all, ...), custom_call_target="tpu_custom_call" | custom-call | tf_op jit(solution)/shard_map/decode/pallas_call | solution.py:542

commit v4 on v3

--- a/solution.py
+++ b/solution.py
@@ -225,9 +225,9 @@
         acc[head, :, HALF:] = first[:, HALF:] + second
         scores = upcoming
 
-    def attend(first, second):
-        keys = jnp.concatenate([kall[first].reshape(HALF, HD), kall[second].reshape(HALF, HD)], axis=0)
-        values = jnp.concatenate([vall[first], vall[second]], axis=1)
+    def attend(*taken):
+        keys = jnp.concatenate([kall[index].reshape(HALF, HD) for index in taken], axis=0)
+        values = jnp.concatenate([vall[index] for index in taken], axis=1)
         scores = dot_nt(keys, query(0))
         for head in range(GROUP):
             upcoming = dot_nt(keys, query(head + 1)) if head + 1 < GROUP else None
@@ -269,46 +269,23 @@
         send_pages(kind)
 
     edge = chip == chips - 1
-    second_turn = jnp.where(edge, 2, 0)
-    far_turn = jnp.where(chip == 0, 1, chip)
-
-    @pl.loop(0, core + jnp.maximum(2 * chip, 2))
-    def _(step):
-        turn = step - core
-
-        @pl.when(turn == 0)
-        def _():
-            arrive(1, 0)
-            arrive(2, 0)
-            send_pages(0)
-
-        @pl.when(turn == second_turn)
-        def _():
-            arrive(1, 1)
-            arrive(2, 1)
-            forward_pages(1)
-            forward_pages(2)
-
-        @pl.when(turn == far_turn)
-        def _():
-            arrive(3, 0)
-            arrive(3, 1)
-            forward_pages(3)
-
+    turns = jnp.maximum(2 * chip, 2)
+    visits = turns // 2
+
+    def ready(turn, active):
         both = edge & (turn >= 0) & (turn < 4)
         single = jnp.where(turn < 0, 0, jnp.where(turn < 2, 1, 3))
         single = jnp.where(edge & (turn >= 4), 3, single)
         kinds = (jnp.where(both, 1, single), jnp.where(both, 2, single))
         halves = (jnp.where(both, turn // 2, 0), jnp.where(both, turn // 2, 1))
         straight = (turn >= 0) & (turn % 2 == 0)
-        wanted = (turn < 0) | (turn < 2 * chip)
         indices = []
         for kind, half in zip(kinds, halves):
             move = jnp.where(kind == 1, chips - 1, jnp.where(kind == 2, 1, jnp.where(kind == 3, 2, 0)))
             index = (lax.rem(chip + move, chips) * 2 + jnp.where(straight, core, 1 - core)) * 2 + half
             indices.append(index)
 
-            @pl.when(wanted & jnp.logical_not(straight))
+            @pl.when(active & jnp.logical_not(straight))
             def _():
                 pltpu.make_async_remote_copy(
                     src_ref=part(own, 0), dst_ref=part(passed.at[kind], half),
@@ -318,9 +295,51 @@
                 kall[index] = passed[kind, 0, pl.ds(half * SLABS, SLABS)]
                 vall[index, :HD, :] = passed[kind, 1, pl.ds(half * SLABS, SLABS)].reshape(HALF, HD).T
 
-        @pl.when(wanted)
+        return indices
+
+    @pl.loop(0, core + 1 + visits)
+    def _(step):
+        visit = step - core
+
+        @pl.when(visit == 0)
+        def _():
+            send_pages(0)
+            arrive(1, 0)
+            arrive(2, 0)
+
+        @pl.when(visit == jnp.where(edge, 1, 0))
+        def _():
+            arrive(1, 1)
+            arrive(2, 1)
+            forward_pages(1)
+            forward_pages(2)
+
+        @pl.when(visit == jnp.where(edge, 2, 1))
+        def _():
+            arrive(3, 0)
+            arrive(3, 1)
+            forward_pages(3)
+
+        paired = (visit >= 1) & (visit < visits)
+        turn = jnp.where(visit <= 0, visit, jnp.where(paired, 2 * visit - 1, turns - 1))
+        wanted = (turn < 0) | (turn < 2 * chip)
+        indices = ready(turn, wanted)
+
+        @pl.when(wanted & jnp.logical_not(paired))
         def _():
             attend(*indices)
+
+        @pl.when(paired)
+        def _():
+            after = turn + 1
+            both = edge & (after < 4)
+            kinds = (jnp.where(both, 1, 3), jnp.where(both, 2, 3))
+            halves = (jnp.where(both, 1, 0), 1)
+            more = []
+            for kind, half in zip(kinds, halves):
+                move = jnp.where(kind == 1, chips - 1, jnp.where(kind == 2, 1, 2))
+                more.append((lax.rem(chip + move, chips) * 2 + core) * 2 + half)
+            attend(*indices, *more)
 
     for head in range(GROUP):
         state = acc[head]
@@ -387,7 +406,6 @@
 
 
 def decode_kernel(
-    gang,
     table_hbm, length_hbm, pages, q_all, new_part, new_v, early_ref, total_ref,
     q_ref, karch_ref, varch_ref,
     final_ref, out_ref,
@@ -407,35 +425,43 @@
     position = lax.broadcasted_iota(jnp.int32, (ROWS, CTX), 1)
     cut = 8
 
-    @pl.loop(0, REQS // gang)
-    def _(turn):
-        scores, extras = [], []
-        for g in range(gang):
-            r = turn * gang + g
-            q = q_all[r]
-            parts = []
-            for b in range(MAXPG // cut):
-                keys = jnp.concatenate([pages[table_ref[r, b * cut + i], :PAGE] for i in range(cut)], axis=0)
-                parts.append(dot_nt(q, keys))
-            scores.append(jnp.where(position < length_ref[r], jnp.concatenate(parts, axis=1), LOW))
-            extras.append(new_part[r])
-        for g in range(gang):
-            r = turn * gang + g
-            top = jnp.maximum(
-                jnp.max(scores[g], axis=1, keepdims=True), jnp.max(extras[g], axis=1, keepdims=True)
-            )
-            weights = jnp.exp2((scores[g] - top) * SCALE)
-            extra = jnp.exp2((extras[g] - top) * SCALE)
-            total = jnp.sum(weights, axis=1, keepdims=True) + jnp.sum(extra, axis=1, keepdims=True)
-            weights = weights.astype(jnp.bfloat16)
-            summed = dot_nn(extra.astype(jnp.bfloat16), new_v[...])
-            for b in range(MAXPG // cut):
-                values = jnp.concatenate([pages[table_ref[r, b * cut + i], PAGE:] for i in range(cut)], axis=0)
-                summed += dot_nn(weights[:, b * cut * PAGE:(b + 1) * cut * PAGE], values)
-            result = summed / total
-            out_ref[r] = jnp.concatenate(
-                [result[h * STEPS:(h + 1) * STEPS] for h in range(GROUP)], axis=1
-            ).astype(jnp.bfloat16)
+    def gather(r, b, low):
+        return jnp.concatenate(
+            [pages[table_ref[r, b * cut + i], low:low + PAGE] for i in range(cut)], axis=0
+        )
+
+    def score(r):
+        q = q_all[r]
+        parts = [dot_nt(q, gather(r, b, 0)) for b in range(MAXPG // cut)]
+        return jnp.concatenate(parts, axis=1)
+
+    def weigh(r, scores):
+        scores = jnp.where(position < length_ref[r], scores, LOW)
+        extra = new_part[r]
+        top = jnp.maximum(jnp.max(scores, axis=1, keepdims=True), jnp.max(extra, axis=1, keepdims=True))
+        weights = jnp.exp2((scores - top) * SCALE)
+        extra = jnp.exp2((extra - top) * SCALE)
+        total = jnp.sum(weights, axis=1, keepdims=True) + jnp.sum(extra, axis=1, keepdims=True)
+        return weights.astype(jnp.bfloat16), extra.astype(jnp.bfloat16), total
+
+    def combine(r, weights, extra, total):
+        summed = dot_nn(extra, new_v[...])
+        for b in range(MAXPG // cut):
+            summed += dot_nn(weights[:, b * cut * PAGE:(b + 1) * cut * PAGE], gather(r, b, PAGE))
+        result = summed / total
+        out_ref[r] = jnp.concatenate(
+            [result[h * STEPS:(h + 1) * STEPS] for h in range(GROUP)], axis=1
+        ).astype(jnp.bfloat16)
+
+    ahead = score(0)
+    waiting = None
+    for r in range(REQS):
+        upcoming = score(r + 1) if r + 1 < REQS else None
+        weighed = weigh(r, ahead)
+        if waiting is not None:
+            combine(r - 1, *waiting)
+        waiting, ahead = weighed, upcoming
+    combine(REQS - 1, *waiting)
 
     loads[0].wait()
 
@@ -540,7 +566,7 @@
         in_hbm(step_values),
     )
     return pl.pallas_call(
-        functools.partial(decode_kernel, REQS),
+        decode_kernel,
         out_shape=(
             jax.ShapeDtypeStruct((1, TOK, GROUP * HD), bf16),
             jax.ShapeDtypeStruct((REQS, STEPS, GROUP * HD), bf16),

time: 33.6 us -> 32.4 us (0.964)
  Pallas kernels: 32.8 us -> 31.4 us
    pallas_call x1, Pallas kernels: 26.5 us -> 25.8 us  [on_device(): pl.pallas_call(functools.partial(prefill_kernel, chips, sections), out_sh...]
    pallas_call x1, Pallas kernels: 6.26 us -> 5.62 us  [on_device(): pl.pallas_call(decode_kernel, out_shape=(jax.ShapeDtypeStruct((1, TOK, GR...]
where the time goes in v4:
time: 32.4 us; the launch traced here: 32.2 us
  Pallas kernels  31.4 us (97%)
  between operations  0.8 us (2%)
    pallas_call x1, Pallas kernels, on_device(): pl.pallas_call(functools.partial(prefill_kernel, chips, sections), out_sh...  25.8 us
    pallas_call x1, Pallas kernels, on_device(): pl.pallas_call(decode_kernel, out_shape=(jax.ShapeDtypeStruct((1, TOK, GR...  5.62 us

profile of v4, /device:TPU:120, one launch (start us, length us, event | category | flops | bytes accessed | tf_op | source)
XLA Modules:
  0.0 32.2 jit_solution(11645650264589068683)
XLA Ops:
  0.6 25.8 %prefill.1 = (bf16[1,512,1024]{2,1,0:T(8,128)(2,1)S(1)}, f32[8,512]{1,0:T(8,128)S(1)}, bf16[16,8,32,128]{3,2,1,0:T(8,128)(2,1)S(1)}, bf16[16,144,256]{2,1,0:T(8,...) custom-call(bf16[1,512,1024]{2,1,0:T(8,128)(2,1)} %q_ref.1, ...), custom_call_target="tpu_custom_call" | custom-call | tf_op jit(solution)/shard_map/prefill/pallas_call | solution.py:523
  26.4 5.6 %decode.1 = (bf16[1,512,1024]{2,1,0:T(8,128)(2,1)}, bf16[16,4,1024]{2,1,0:T(4,128)(2,1)}) custom-call(s32[16,64]{1,0:T(8,128)} %table_hbm.1, s32[16]{0:T(128)} %length_hbm.1, bf16[288,64,128]{2,1,0:T(8,128)(2,1)S(1)} %get-tuple-element.10.pages, bf16[16,32,128]{2,1,0:T(8,128)(2,1)S(1)} %get-tuple-element.11.q_all, ...), custom_call_target="tpu_custom_call" | custom-call | tf_op jit(solution)/shard_map/decode/pallas_call | solution.py:568

commit v5 on v4

--- a/solution.py
+++ b/solution.py
@@ -169,11 +169,11 @@
             def _():
                 page_copy(kind, 0, other).start()
 
+    near_table(True).start()
+    near_table(False).start()
     for half in range(2):
         near_copy(True, half).start()
         near_copy(False, half).start()
-    near_table(True).start()
-    near_table(False).start()
 
     @pl.when(core == 0)
     def _():
@@ -255,7 +255,7 @@
             mate_copy(kind, half).start()
             take(kind, half)
 
-    def forward_pages(kind):
+    def fetch_table(kind):
         pltpu.make_async_remote_copy(
             src_ref=table0, dst_ref=tables[kind], send_sem=tsend.at[2], recv_sem=trecv.at[kind],
             device_id=place(section, mate), device_id_type=MESH,
@@ -265,6 +265,8 @@
             def _():
                 relay_table(kind == 1).start()
         local_owners(kind).start()
+
+    def forward_pages(kind):
         local_owners(kind).wait()
         send_pages(kind)
 
@@ -306,6 +308,8 @@
             send_pages(0)
             arrive(1, 0)
             arrive(2, 0)
+            fetch_table(1)
+            fetch_table(2)
 
         @pl.when(visit == jnp.where(edge, 1, 0))
         def _():
@@ -316,6 +320,7 @@
 
         @pl.when(visit == jnp.where(edge, 2, 1))
         def _():
+            fetch_table(3)
             arrive(3, 0)
             arrive(3, 1)
             forward_pages(3)

time: 32.4 us -> 31.2 us (0.963)
  Pallas kernels: 31.4 us -> 30.2 us
    pallas_call x1, Pallas kernels: 25.8 us -> 24.6 us  [on_device(): pl.pallas_call(functools.partial(prefill_kernel, chips, sections), out_sh...]
where the time goes in v5:
time: 31.2 us; the launch traced here: 31 us
  Pallas kernels  30.2 us (97%)
  between operations  0.8 us (3%)
    pallas_call x1, Pallas kernels, on_device(): pl.pallas_call(functools.partial(prefill_kernel, chips, sections), out_sh...  24.6 us
    pallas_call x1, Pallas kernels, on_device(): pl.pallas_call(decode_kernel, out_shape=(jax.ShapeDtypeStruct((1, TOK, GR...  5.61 us

profile of v5, /device:TPU:120, one launch (start us, length us, event | category | flops | bytes accessed | tf_op | source)
XLA Modules:
  0.0 31.0 jit_solution(505097812295079211)
XLA Ops:
  0.6 24.6 %prefill.1 = (bf16[1,512,1024]{2,1,0:T(8,128)(2,1)S(1)}, f32[8,512]{1,0:T(8,128)S(1)}, bf16[16,8,32,128]{3,2,1,0:T(8,128)(2,1)S(1)}, bf16[16,144,256]{2,1,0:T(8,...) custom-call(bf16[1,512,1024]{2,1,0:T(8,128)(2,1)} %q_ref.1, ...), custom_call_target="tpu_custom_call" | custom-call | tf_op jit(solution)/shard_map/prefill/pallas_call | solution.py:528
  25.2 5.6 %decode.1 = (bf16[1,512,1024]{2,1,0:T(8,128)(2,1)}, bf16[16,4,1024]{2,1,0:T(4,128)(2,1)}) custom-call(s32[16,64]{1,0:T(8,128)} %table_hbm.1, s32[16]{0:T(128)} %length_hbm.1, bf16[288,64,128]{2,1,0:T(8,128)(2,1)S(1)} %get-tuple-element.10.pages, bf16[16,32,128]{2,1,0:T(8,128)(2,1)S(1)} %get-tuple-element.11.q_all, ...), custom_call_target="tpu_custom_call" | custom-call | tf_op jit(solution)/shard_map/decode/pallas_call | solution.py:573
